TPU v7x, 512 devices: a whole 4x8x8 slice. The times are simulated.
512 devices in a mesh: dp: 4 (over x), expert: 128 (over z, y, core).
Axes of the slice: x: 4, y: 8, z: 8, core: 2. Of those that a mesh axis runs over, the one named last changes fastest.
Arguments:
- tokens: bfloat16 [12288, 1024], P(('dp', 'expert')), may hold values from -6 to 6
- grad_out: bfloat16 [12288, 1024], P(('dp', 'expert')), may hold values from -6 to 6
- expert_ids: int32 [12288, 8], P(('dp', 'expert')), may hold values from 0 to 127, all different within a row; in each aligned block of 24 rows (0 to 23, 24 to 47, ...) at most 2 rows name the same one
- gates: float32 [12288, 8], P(('dp', 'expert')), may hold values from 0.05 to 0.5
- w_in: bfloat16 [128, 1024, 2, 512], P('expert', None, None, 'dp'), may hold values from -0.1875 to 0.1875
- w_out: bfloat16 [128, 512, 1024], P('expert', 'dp'), may hold values from -0.25 to 0.25
Outputs:
- mixed: bfloat16 [12288, 1024], P(('dp', 'expert'))
- grad_tokens: bfloat16 [12288, 1024], P(('dp', 'expert'))
- grad_gates: float32 [12288, 8], P(('dp', 'expert'))
- grad_w_in: float32 [128, 1024, 2, 512], P('expert', None, None, 'dp')
- grad_w_out: float32 [128, 512, 1024], P('expert', 'dp')
Inputs may be any that keep to these rules, and one draw needn't show every extreme that they name: `expert_ids`: each token names 8 different experts; the rows of one device name no expert more than 2 times, a bound that some block reaches.
All inputs are finite; a program needn't handle non-finite values.
Results may differ from a plain program's by a relative error of at most 0.012.
Values may be sent and summed in bfloat16 or wider, within the bound.
No kernel may reach another device: no remote copies, remote signals or barrier semaphores. Data moves between devices by JAX's collectives and lax.ppermute only.
A program may use at most 64 MiB of HBM per device.

v0:
```python
import jax
import jax.numpy as jnp
from jax import lax
from jax.sharding import PartitionSpec as P


def forward_part(rows, weight_in, weight_out):
    model_width = rows.shape[1]
    hidden_width = weight_out.shape[0]
    flat_in = weight_in.reshape(model_width, 2 * hidden_width)
    preact = jnp.dot(rows, flat_in, preferred_element_type=jnp.float32)
    gate_part = preact[:, :hidden_width]
    up_part = preact[:, hidden_width:]
    activated = gate_part * jax.nn.sigmoid(gate_part)
    hidden = (activated * up_part).astype(jnp.bfloat16)
    result = jnp.dot(hidden, weight_out, preferred_element_type=jnp.float32).astype(jnp.bfloat16)
    return (preact, hidden, result)


def backward_part(rows, preact, hidden, grad_rows, weight_in, weight_out):
    model_width = rows.shape[1]
    hidden_width = weight_out.shape[0]
    flat_in = weight_in.reshape(model_width, 2 * hidden_width)
    gate_part = preact[:, :hidden_width]
    up_part = preact[:, hidden_width:]
    sigmoid_gate = jax.nn.sigmoid(gate_part)
    activated = gate_part * sigmoid_gate
    back_grad = jnp.einsum("sd,hd->sh", grad_rows, weight_out, preferred_element_type=jnp.float32)
    grad_gate = back_grad * up_part * (sigmoid_gate * (1.0 + gate_part * (1.0 - sigmoid_gate)))
    grad_up = back_grad * activated
    grad_pre = jnp.concatenate([grad_gate, grad_up], axis=1).astype(jnp.bfloat16)
    grad_rows_in = jnp.einsum(
        "sk,dk->sd", grad_pre, flat_in, preferred_element_type=jnp.float32
    ).astype(jnp.bfloat16)
    grad_weight_in = jnp.einsum("sd,sk->dk", rows, grad_pre, preferred_element_type=jnp.float32)
    grad_weight_out = jnp.einsum("sh,sd->hd", hidden, grad_rows, preferred_element_type=jnp.float32)
    return (grad_rows_in, grad_weight_in, grad_weight_out)


def per_device(tokens, grad_out, expert_ids, gates, w_in, w_out):
    count_tok, model_width = tokens.shape
    per_token = expert_ids.shape[1]
    groups = lax.axis_size("expert")
    capacity = min(count_tok, 3 * count_tok * per_token // (2 * groups))
    row_count = count_tok * per_token
    flat_ids = expert_ids.reshape(-1)
    onehot = (flat_ids[:, None] == jnp.arange(groups, dtype=jnp.int32)[None, :]).astype(jnp.int32)
    order_rank = jnp.sum((jnp.cumsum(onehot, axis=0) - onehot) * onehot, axis=1)
    slot_of_row = flat_ids * capacity + order_rank
    inverse = (
        jnp.full((groups * capacity,), row_count, jnp.int32)
        .at[slot_of_row]
        .set(jnp.arange(row_count, dtype=jnp.int32))
    )
    token_of_slot = jnp.where(inverse < row_count, inverse // per_token, count_tok)
    tokens_padded = jnp.concatenate([tokens, jnp.zeros((1, model_width), jnp.bfloat16)], axis=0)
    grad_padded = jnp.concatenate([grad_out, jnp.zeros((1, model_width), jnp.bfloat16)], axis=0)
    gates_padded = jnp.concatenate([gates.reshape(-1), jnp.zeros((1,), jnp.float32)], axis=0)
    send_rows = tokens_padded[token_of_slot].reshape(groups, capacity, model_width)
    slot_gate = gates_padded[inverse]
    send_grads = (slot_gate[:, None] * grad_padded[token_of_slot].astype(jnp.float32)).astype(
        jnp.bfloat16
    )
    send_grads = send_grads.reshape(groups, capacity, model_width)
    full_in, full_out = (
        lax.all_gather(w_in, "dp", axis=3, tiled=True),
        lax.all_gather(w_out, "dp", axis=1, tiled=True),
    )
    weight_in = full_in[0]
    weight_out = full_out[0]
    hidden_width = weight_out.shape[0]
    arrived_rows = lax.all_to_all(send_rows, "expert", split_axis=0, concat_axis=0, tiled=True)
    rows = arrived_rows.reshape(groups * capacity, model_width)
    preact, hidden, result = forward_part(rows, weight_in, weight_out)
    back_out = lax.all_to_all(
        result.reshape(groups, capacity, model_width),
        "expert",
        split_axis=0,
        concat_axis=0,
        tiled=True,
    )
    arrived_grads = lax.all_to_all(send_grads, "expert", split_axis=0, concat_axis=0, tiled=True)
    grad_rows = arrived_grads.reshape(groups * capacity, model_width)
    grad_rows_in, grad_weight_in, grad_weight_out = backward_part(
        rows, preact, hidden, grad_rows, weight_in, weight_out
    )
    back_grads = lax.all_to_all(
        grad_rows_in.reshape(groups, capacity, model_width),
        "expert",
        split_axis=0,
        concat_axis=0,
        tiled=True,
    )
    out_rows = back_out.reshape(groups * capacity, model_width)[slot_of_row].reshape(
        count_tok, per_token, model_width
    )
    mixed = jnp.sum(gates[:, :, None] * out_rows.astype(jnp.float32), axis=1).astype(jnp.bfloat16)
    grad_gates = jnp.einsum("td,tkd->tk", grad_out, out_rows, preferred_element_type=jnp.float32)
    route_dx = back_grads.reshape(groups * capacity, model_width)[slot_of_row].reshape(
        count_tok, per_token, model_width
    )
    grad_tokens = jnp.sum(route_dx.astype(jnp.float32), axis=1).astype(jnp.bfloat16)
    grad_in_shard, grad_out_shard = (
        lax.psum_scatter(
            grad_weight_in.reshape(1, model_width, 2, hidden_width).astype(jnp.bfloat16),
            "dp",
            scatter_dimension=3,
            tiled=True,
        ).astype(jnp.float32),
        lax.psum_scatter(
            grad_weight_out[None].astype(jnp.bfloat16), "dp", scatter_dimension=1, tiled=True
        ).astype(jnp.float32),
    )
    return (mixed, grad_tokens, grad_gates, grad_in_shard, grad_out_shard)


def solution(mesh):
    in_specs = (
        P(("dp", "expert"), None),
        P(("dp", "expert"), None),
        P(("dp", "expert"), None),
        P(("dp", "expert"), None),
        P("expert", None, None, "dp"),
        P("expert", "dp", None),
    )
    out_specs = (
        P(("dp", "expert"), None),
        P(("dp", "expert"), None),
        P(("dp", "expert"), None),
        P("expert", None, None, "dp"),
        P("expert", "dp", None),
    )
    return jax.shard_map(
        per_device, mesh=mesh, in_specs=in_specs, out_specs=out_specs, check_vma=False
    )
```

profile of v0, /device:TPU:1, one launch (start us, length us, event | category | flops | bytes accessed | tf_op | source)
XLA Modules:
  0.0 203.7 jit_solution(10803530581924078877)
XLA Ops:
  7.2 0.7 all-gather.3.cloned.1.call-update
  7.9 0.8 copy.26
  8.7 0.7 broadcast_multiply_fusion
  10.0 0.8 concatenate.13
  11.0 1.2 scatter_custom_fusion
  12.2 1.2 gather_fusion
  13.4 1.0 reshape.99
  14.4 18.4 %all-to-all-start = ((bf16[128,2,1024]{2,1,0:T(2,128)(2,1)}), bf16[128,2,1024]{2,1,0:T(2,128)(2,1)S(1)}, u32[]{:S(2)}, u32[]{:S(2)}) async-start(bf16[128,2,1024]{2,1,0:T(2,128)(2,1)} %reshape.99), calls=%async_computation | async-start | bytes 1048576 | tf_op jit(solution)/shard_map/all_to_all | solution.py:72
  32.9 0.7 all-gather.5.cloned.1.call-update
  33.6 1.2 gather_fusion.3
  34.8 0.7 reshape.110
  35.7 1.9 gather_fusion.2
  37.8 1.2 multiply_convert_fusion
  39.0 14.4 %all-to-all-done = bf16[128,2,1024]{2,1,0:T(2,128)(2,1)S(1)} async-done(((bf16[128,2,1024]{2,1,0:T(2,128)(2,1)}), bf16[128,2,1024]{2,1,0:T(2,128)(2,1)S(1)}, u32[]{:S(2)}, u32[]{:S(2)}) %all-to-all-start) | async-done | bytes 524320 | tf_op jit(solution)/shard_map/all_to_all | solution.py:72
  53.4 5.4 %all-to-all-start.2 = ((bf16[128,2,1024]{2,1,0:T(2,128)(2,1)}), bf16[128,2,1024]{2,1,0:T(2,128)(2,1)S(1)}, u32[]{:S(2)}, u32[]{:S(2)}) async-start(bf16[128,2,1024]{2,1,0:T(2,128)(2,1)} %multiply_convert_fusion), calls=%async_computation.2 | async-start | bytes 1048576 | tf_op jit(solution)/shard_map/all_to_all | solution.py:82
  58.9 0.2 reshape.100
  59.1 20.3 %all-to-all-done.2 = bf16[128,2,1024]{2,1,0:T(2,128)(2,1)S(1)} async-done(((bf16[128,2,1024]{2,1,0:T(2,128)(2,1)}), bf16[128,2,1024]{2,1,0:T(2,128)(2,1)S(1)}, u32[]{:S(2)}, u32[]{:S(2)}) %all-to-all-start.2) | async-done | bytes 524320 | tf_op jit(solution)/shard_map/all_to_all | solution.py:82
  79.4 0.2 reshape.105
  79.6 2.1 %copy.40 = bf16[128,8,2,512]{3,1,2,0:T(8,128)(2,1)S(1)} copy(bf16[128,8,2,512]{3,2,1,0:T(2,128)(2,1)} %bitcast.57) | data formatting | bytes 4194304
  81.8 1.7 fusion.17
  83.5 20.3 %all-gather.5.cloned.1.call-done = bf16[1,512,1024]{2,1,0:T(8,128)(2,1)} async-done(((bf16[1,128,1024]{2,1,0:T(8,128)(2,1)}), bf16[1,512,1024]{2,1,0:T(8,128)(2,1)}) %all-gather.5.cloned.1.call-update) | async-done | bytes 1048592 | tf_op jit(solution)/shard_map/all_gather | solution.py:67
  103.7 3.0 %multiply_convert_fusion.2 = (bf16[256,512]{1,0:T(8,128)(2,1)}, bf16[256,512]{1,0:T(8,128)(2,1)}, bf16[256,512]{1,0:T(8,128)(2,1)S(1)}) fusion(f32[256,1024]{1,0:T(8,128)} %fusion.17, bf16[256,1024]{1,0:T(8,128)(2,1)S(1)} %reshape.105, bf16[1,512,1024]{2,1,0:T(8,128)(2,1)} %all-gather.5.cloned.1.call-done), kind=kOutput, calls=%fused_computation.19 | convolution fusion | flops 270401536 | bytes 3407872 | tf_op jit(solution)/shard_map/sd,hd->sh/dot_general | solution.py:28
  106.7 1.4 fusion
  108.2 0.2 reduce-scatter.7.cloned.1.call-start
  108.4 1.1 fusion.8
  109.5 1.0 copy.37
  110.5 3.1 %convert_bitcast_fusion = bf16[1,1024,2,512]{3,1,2,0:T(8,128)(2,1)} fusion(bf16[2,512,256]{2,1,0:T(8,128)(2,1)} %bitcast.59, bf16[256,1024]{1,0:T(8,128)(2,1)S(1)} %reshape.100), kind=kOutput, calls=%fused_computation.6 | convolution fusion | flops 537919488 | bytes 3145728 | tf_op jit(solution)/shard_map/sd,sk->dk/dot_general | solution.py:35
  113.6 6.2 %copy.38 = bf16[1,1024,2,512]{1,2,0,3:T(2,128)(2,1)} copy(bf16[1,1024,2,512]{3,1,2,0:T(8,128)(2,1)} %convert_bitcast_fusion) | data formatting | bytes 4194304
  119.9 3.5 %copy.41 = bf16[64,8,2,1024]{3,1,2,0:T(8,128)(2,1)} copy(bf16[64,8,2,1024]{3,2,1,0:T(2,128)(2,1)} %bitcast.56) | data formatting | bytes 4194304
  123.4 1.7 convolution_convert_fusion.1
  125.2 1.0 reshape.101
  126.1 15.2 %all-to-all-start.1 = ((bf16[128,2,1024]{2,1,0:T(2,128)(2,1)}), bf16[128,2,1024]{2,1,0:T(2,128)(2,1)S(1)}, u32[]{:S(2)}, u32[]{:S(2)}) async-start(bf16[128,2,1024]{2,1,0:T(2,128)(2,1)} %reshape.101), calls=%async_computation.1 | async-start | bytes 1048576 | tf_op jit(solution)/shard_map/all_to_all | solution.py:75
  141.3 1.7 convolution_convert_fusion.2
  143.0 1.0 reshape.106
  144.0 17.9 %all-to-all-done.1 = bf16[128,2,1024]{2,1,0:T(2,128)(2,1)S(1)} async-done(((bf16[128,2,1024]{2,1,0:T(2,128)(2,1)}), bf16[128,2,1024]{2,1,0:T(2,128)(2,1)S(1)}, u32[]{:S(2)}, u32[]{:S(2)}) %all-to-all-start.1) | async-done | bytes 524320 | tf_op jit(solution)/shard_map/all_to_all | solution.py:75
  161.9 5.4 %all-to-all-start.3 = ((bf16[128,2,1024]{2,1,0:T(2,128)(2,1)}), bf16[128,2,1024]{2,1,0:T(2,128)(2,1)S(1)}, u32[]{:S(2)}, u32[]{:S(2)}) async-start(bf16[128,2,1024]{2,1,0:T(2,128)(2,1)} %reshape.106), calls=%async_computation.3 | async-start | bytes 1048576 | tf_op jit(solution)/shard_map/all_to_all | solution.py:87
  167.3 0.2 reshape.102
  167.5 1.0 gather_fusion.1
  168.5 19.3 %all-to-all-done.3 = bf16[128,2,1024]{2,1,0:T(2,128)(2,1)S(1)} async-done(((bf16[128,2,1024]{2,1,0:T(2,128)(2,1)}), bf16[128,2,1024]{2,1,0:T(2,128)(2,1)S(1)}, u32[]{:S(2)}, u32[]{:S(2)}) %all-to-all-start.3) | async-done | bytes 524320 | tf_op jit(solution)/shard_map/all_to_all | solution.py:87
  188.1 1.0 gather_fusion.4
  189.1 0.3 fusion.6
  189.4 0.7 copy.34
  190.1 0.9 bitcast_reduce_fusion
  191.0 0.9 multiply_reduce_fusion
  191.9 1.8 convert_element_type.65
  193.7 1.4 reshape.166
  195.1 0.5 copy.39
  195.7 1.5 copy.32
  (38 shorter events, 1.6 us)
Async XLA Ops:
  7.2 72.4 %all-gather.3.cloned.1.call-start = ((), (), s32[]{:S(2)}) async-start(), calls=%async_computation.6 | async-start | bytes 2621440 | tf_op jit(solution)/shard_map/all_gather | solution.py:66
  13.4 20.2 %copy-start.1 = (bf16[24,1024]{1,0:T(8,128)(2,1)S(1)}, bf16[24,1024]{1,0:T(8,128)(2,1)}, u32[]{:S(2)}) copy-start(bf16[24,1024]{1,0:T(8,128)(2,1)} %param.7) | copy-start | bytes 147460
  14.4 39.0 %all-to-all-start = ((bf16[128,2,1024]{2,1,0:T(2,128)(2,1)}), bf16[128,2,1024]{2,1,0:T(2,128)(2,1)S(1)}, u32[]{:S(2)}, u32[]{:S(2)}) async-start(bf16[128,2,1024]{2,1,0:T(2,128)(2,1)} %reshape.99), calls=%async_computation | async-start | bytes 1048576 | tf_op jit(solution)/shard_map/all_to_all | solution.py:72
  32.8 70.9 %all-gather.5.cloned.1.call-start = ((), (), s32[]{:S(2)}) async-start(), calls=%async_computation.7 | async-start | bytes 1310720 | tf_op jit(solution)/shard_map/all_gather | solution.py:67
  33.6 1.8 copy-start.2
  53.4 26.0 %all-to-all-start.2 = ((bf16[128,2,1024]{2,1,0:T(2,128)(2,1)}), bf16[128,2,1024]{2,1,0:T(2,128)(2,1)S(1)}, u32[]{:S(2)}, u32[]{:S(2)}) async-start(bf16[128,2,1024]{2,1,0:T(2,128)(2,1)} %multiply_convert_fusion), calls=%async_computation.2 | async-start | bytes 1048576 | tf_op jit(solution)/shard_map/all_to_all | solution.py:82
  58.8 133.1 %reduce-scatter.5.cloned.1.call-start = ((), (), s32[]{:S(2)}) async-start(), calls=%async_computation.8 | async-start | bytes 1310720 | tf_op jit(solution)/shard_map/reduce_scatter | solution.py:110
  108.2 85.5 %reduce-scatter.7.cloned.1.call-start = ((), (), s32[]{:S(2)}) async-start(), calls=%async_computation.9 | async-start | bytes 2621440
  125.1 16.2 %copy-start = (bf16[256,512]{1,0:T(8,128)(2,1)S(1)}, bf16[256,512]{1,0:T(8,128)(2,1)}, u32[]{:S(2)}) copy-start(bf16[256,512]{1,0:T(8,128)(2,1)} %get-tuple-element.20) | copy-start | bytes 786436
  126.1 35.7 %all-to-all-start.1 = ((bf16[128,2,1024]{2,1,0:T(2,128)(2,1)}), bf16[128,2,1024]{2,1,0:T(2,128)(2,1)S(1)}, u32[]{:S(2)}, u32[]{:S(2)}) async-start(bf16[128,2,1024]{2,1,0:T(2,128)(2,1)} %reshape.101), calls=%async_computation.1 | async-start | bytes 1048576 | tf_op jit(solution)/shard_map/all_to_all | solution.py:75
  161.9 26.0 %all-to-all-start.3 = ((bf16[128,2,1024]{2,1,0:T(2,128)(2,1)}), bf16[128,2,1024]{2,1,0:T(2,128)(2,1)S(1)}, u32[]{:S(2)}, u32[]{:S(2)}) async-start(bf16[128,2,1024]{2,1,0:T(2,128)(2,1)} %reshape.106), calls=%async_computation.3 | async-start | bytes 1048576 | tf_op jit(solution)/shard_map/all_to_all | solution.py:87
Sparse Core Ops, SparseCore 0:
  10.1 60.4 all-gather.2
  72.6 31.0 all-gather.4
  108.3 28.0 reduce-scatter.4
  139.3 36.9 reduce-scatter.6
where the time goes:
time: 205 us; the launch traced here: 204 us
  waiting for transfers between devices  93.6 us (46%)
  starting transfers between devices  44.7 us (22%)
  local copies, waits for them, and re-layouts  31.2 us (15%)
  between operations  14 us (7%)
  matrix products  13 us (6%)
  other arithmetic  7.19 us (4%)
    all_to_all x1, waiting for transfers between devices, per_device(): lax.all_to_all(send_grads, 'expert', split_axis=0, concat_axis=0, tiled=T...  20.3 us
    all_gather x1, waiting for transfers between devices, per_device(): lax.all_gather(w_out, 'dp', axis=1, tiled=True)  20.3 us
    all_to_all x1, waiting for transfers between devices, per_device(): lax.all_to_all(grad_rows_in.reshape(groups, capacity, model_width), 'expe...  19.3 us
    all_to_all x1, starting transfers between devices, per_device(): lax.all_to_all(send_rows, 'expert', split_axis=0, concat_axis=0, tiled=True)  18.4 us
    all_to_all x1, waiting for transfers between devices, per_device(): lax.all_to_all(result.reshape(groups, capacity, model_width), 'expert', s...  17.9 us
    unnamed x15, local copies, waits for them, and re-layouts  16.2 us
    all_to_all x1, starting transfers between devices, per_device(): lax.all_to_all(result.reshape(groups, capacity, model_width), 'expert', s...  15.2 us
    all_to_all x1, waiting for transfers between devices, per_device(): lax.all_to_all(send_rows, 'expert', split_axis=0, concat_axis=0, tiled=True)  14.4 us
  transfers between devices with their start and end apart: 8, of which 5 were waited for; matrix products, arithmetic and copies ran while one was open for 21% of the time, Pallas kernels for 0%

commit v1 on v0

v1 whole, which is shorter than its diff:
```python
import jax
import jax.numpy as jnp
from jax import lax
from jax.experimental import pallas as pl
from jax.experimental.pallas import tpu as pltpu
from jax.sharding import PartitionSpec as P

BF16 = jnp.bfloat16
F32 = jnp.float32
SLOTS = 2
VMEM_LIMIT = 48 * 1024 * 1024


def routing(ids, gates, groups):
    count_tok, per_token = ids.shape
    slots = groups * SLOTS
    lane = lax.broadcasted_iota(jnp.int32, (count_tok, slots), 1)
    expert = lane // SLOTS
    place = lane % SLOTS
    named = jnp.zeros((count_tok, slots), F32)
    gate = jnp.zeros((count_tok, slots), F32)
    for k in range(per_token):
        hit = ids[:, k : k + 1] == expert
        named = jnp.where(hit, 1.0, named)
        gate = jnp.where(hit, gates[:, k : k + 1], gate)
    row = lax.broadcasted_iota(jnp.int32, (count_tok, count_tok), 0)
    col = lax.broadcasted_iota(jnp.int32, (count_tok, count_tok), 1)
    earlier = (col < row).astype(BF16)
    rank = jnp.dot(earlier, named.astype(BF16), preferred_element_type=F32)
    held = jnp.where(rank == place.astype(F32), named, 0.0)
    return held, held * gate, expert


def three_parts(x):
    high = x.astype(BF16)
    rest = x - high.astype(F32)
    mid = rest.astype(BF16)
    low = (rest - mid.astype(F32)).astype(BF16)
    return high, mid, low


def dispatch_kernel(tokens_ref, grad_ref, ids_ref, gates_ref, send_ref):
    model = tokens_ref.shape[1]
    groups = send_ref.shape[0] // SLOTS
    held, gate, _ = routing(ids_ref[...], gates_ref[...], groups)
    pick = (((0,), (0,)), ((), ()))
    send_ref[:, :model] = lax.dot_general(
        held.astype(BF16), tokens_ref[...], pick, preferred_element_type=F32
    ).astype(BF16)
    grad = grad_ref[...]
    send_ref[:, model:] = lax.dot_general(
        jnp.concatenate(three_parts(gate), axis=0),
        jnp.concatenate([grad, grad, grad], axis=0),
        pick,
        preferred_element_type=F32,
    ).astype(BF16)


def expert_kernel(model, *refs):
    pieces = (len(refs) - 2) // 2
    rows_ref, weights = refs[0], refs[1 : 1 + pieces]
    back_ref, grads = refs[1 + pieces], refs[2 + pieces :]
    rows = rows_ref[:, :model]
    grad_rows = rows_ref[:, model:]
    last = (((1,), (1,)), ((), ()))
    first = (((0,), (0,)), ((), ()))
    result = None
    dx = None
    for w_ref, g_ref in zip(weights, grads):
        wide = w_ref.shape[1]
        width = wide // 2
        w_in = w_ref[:model, :]
        w_out = jnp.concatenate(
            [w_ref[model + i * width : model + (i + 1) * width, :] for i in range(model // wide)], axis=1
        )
        preact = jnp.dot(rows, w_in, preferred_element_type=F32)
        gate_part, up_part = preact[:, :width], preact[:, width:]
        sig = jax.nn.sigmoid(gate_part)
        activated = gate_part * sig
        hidden = (activated * up_part).astype(BF16)
        back = lax.dot_general(grad_rows, w_out, last, preferred_element_type=F32)
        grad_gate = back * up_part * (sig * (1.0 + gate_part * (1.0 - sig)))
        grad_pre = jnp.concatenate([grad_gate, back * activated], axis=1).astype(BF16)
        part = jnp.dot(hidden, w_out, preferred_element_type=F32)
        result = part if result is None else result + part
        part = lax.dot_general(grad_pre, w_in, last, preferred_element_type=F32)
        dx = part if dx is None else dx + part
        g_ref[:model, :] = lax.dot_general(rows, grad_pre, first, preferred_element_type=F32).astype(BF16)
        grad_out = lax.dot_general(hidden, grad_rows, first, preferred_element_type=F32).astype(BF16)
        for i in range(model // wide):
            g_ref[model + i * width : model + (i + 1) * width, :] = grad_out[:, i * wide : (i + 1) * wide]
    back_ref[:, :model] = result.astype(BF16)
    back_ref[:, model:] = dx.astype(BF16)


def combine_kernel(back_ref, grad_ref, ids_ref, gates_ref, mixed_ref, dx_ref, gate_grad_ref):
    model = grad_ref.shape[1]
    groups = back_ref.shape[0] // SLOTS
    ids = ids_ref[...]
    count_tok, per_token = ids.shape
    held, gate, expert = routing(ids, gates_ref[...], groups)
    result = back_ref[:, :model]
    mixed = jnp.dot(jnp.concatenate(three_parts(gate), axis=0), result, preferred_element_type=F32)
    mixed_ref[...] = (
        mixed[:count_tok] + mixed[count_tok : 2 * count_tok] + mixed[2 * count_tok :]
    ).astype(BF16)
    dx_ref[...] = jnp.dot(held.astype(BF16), back_ref[:, model:], preferred_element_type=F32).astype(BF16)
    inner = lax.dot_general(grad_ref[...], result, (((1,), (1,)), ((), ())), preferred_element_type=F32)
    inner = inner * held
    for k in range(per_token):
        hit = ids[:, k : k + 1] == expert
        gate_grad_ref[:, k : k + 1] = jnp.sum(jnp.where(hit, inner, 0.0), axis=1, keepdims=True)


def per_device(tokens, grad_out, expert_ids, gates, w_in, w_out):
    count_tok, model = tokens.shape
    groups = lax.axis_size("expert")
    replicas = lax.axis_size("dp")
    width = w_out.shape[1]
    wide = 2 * width
    params = pltpu.CompilerParams(vmem_limit_bytes=VMEM_LIMIT)

    def shift(x, by):
        return lax.ppermute(x, "dp", [(i, (i + by) % replicas) for i in range(replicas)])

    packed = jnp.concatenate(
        [
            w_in.reshape(model, wide),
            w_out.reshape(width, model // wide, wide).transpose(1, 0, 2).reshape(-1, wide),
        ],
        axis=0,
    )
    order = (0, 1, 3, 2)
    weights = [packed] + [shift(packed, -s) for s in order[1:]]

    send = pl.pallas_call(
        dispatch_kernel,
        out_shape=jax.ShapeDtypeStruct((groups * SLOTS, 2 * model), BF16),
        compiler_params=params,
        name="dispatch",
    )(tokens, grad_out, expert_ids, gates)

    def exchange(x):
        x = x.reshape(groups, SLOTS, 2 * model)
        x = lax.all_to_all(x, "expert", split_axis=0, concat_axis=0, tiled=True)
        return x.reshape(groups * SLOTS, 2 * model)

    arrived = exchange(send)
    back, *grads = pl.pallas_call(
        lambda *refs: expert_kernel(model, *refs),
        out_shape=[jax.ShapeDtypeStruct((groups * SLOTS, 2 * model), BF16)]
        + [jax.ShapeDtypeStruct(packed.shape, BF16)] * replicas,
        compiler_params=params,
        name="expert",
    )(arrived, *weights)
    total = grads[0].astype(F32)
    for s, grad in zip(order[1:], grads[1:]):
        total = total + shift(grad, s).astype(F32)
    returned = exchange(back)
    mixed, grad_tokens, grad_gates = pl.pallas_call(
        combine_kernel,
        out_shape=[
            jax.ShapeDtypeStruct(tokens.shape, BF16),
            jax.ShapeDtypeStruct(tokens.shape, BF16),
            jax.ShapeDtypeStruct(gates.shape, F32),
        ],
        compiler_params=params,
        name="combine",
    )(returned, grad_out, expert_ids, gates)
    grad_w_in = total[:model].reshape(1, model, 2, width)
    grad_w_out = total[model:].reshape(model // wide, width, wide).transpose(1, 0, 2).reshape(1, width, model)
    return mixed, grad_tokens, grad_gates, grad_w_in, grad_w_out


def solution(mesh):
    in_specs = (
        P(("dp", "expert"), None),
        P(("dp", "expert"), None),
        P(("dp", "expert"), None),
        P(("dp", "expert"), None),
        P("expert", None, None, "dp"),
        P("expert", "dp", None),
    )
    out_specs = (
        P(("dp", "expert"), None),
        P(("dp", "expert"), None),
        P(("dp", "expert"), None),
        P("expert", None, None, "dp"),
        P("expert", "dp", None),
    )
    return jax.shard_map(
        per_device, mesh=mesh, in_specs=in_specs, out_specs=out_specs, check_vma=False
    )
```

time: 205 us -> 139 us (0.68)
  waiting for transfers between devices: 93.6 us -> 55.3 us
  local copies, waits for them, and re-layouts: 31.2 us -> 17.6 us
  between operations: 14 us -> 0.83 us
  matrix products: 13 us -> 0 us
  starting transfers between devices: 44.7 us -> 54.5 us
  Pallas kernels: 0 us -> 7.62 us
  other arithmetic: 7.19 us -> 0.46 us
    all_to_all x4 -> x2, waiting for transfers between devices: 71.9 us -> 19 us  [exchange(): x = lax.all_to_all(x, 'expert', split_axis=0, concat_axis=0, tiled=True)]
    ppermute x0 -> x6, waiting for transfers between devices: none -> 36.4 us  [shift(): lax.ppermute(x, 'dp', [(i, (i + by) % replicas) for i in range(replicas)])]
    ppermute x0 -> x6, starting transfers between devices: none -> 20.9 us  [shift(): lax.ppermute(x, 'dp', [(i, (i + by) % replicas) for i in range(replicas)])]
    all_gather x2 -> x0, waiting for transfers between devices: 20.3 us -> none  [the longest x1 20.3 us: per_device(): lax.all_gather(w_out, 'dp', axis=1, tiled=True)]
    dot_general x7 -> x0, matrix products: 13 us -> none  [the longest x1 3.14 us: backward_part(): jnp.einsum('sd,sk->dk', rows, grad_pre, preferred_element_type=jnp.float32)]
    all_to_all x4 -> x2, starting transfers between devices: 44.4 us -> 33.6 us  [exchange(): x = lax.all_to_all(x, 'expert', split_axis=0, concat_axis=0, tiled=True)]
    unnamed x15 -> x28, local copies, waits for them, and re-layouts: 16.2 us -> 6.53 us
    pallas_call x0 -> x3, Pallas kernels: none -> 7.62 us  [the longest x1 5.82 us: per_device(): pl.pallas_call(lambda *refs: expert_kernel(model, *refs), out_shape=[jax....]
  transfers between devices with their start and end apart: 8 -> 8, of which waited for: 5 -> 5; matrix products, arithmetic and copies ran while one was open for 21% -> 4% of each run, Pallas kernels for 0% -> 0%
where the time goes in v1:
time: 139 us; the launch traced here: 136 us
  waiting for transfers between devices  55.3 us (40%)
  starting transfers between devices  54.5 us (39%)
  local copies, waits for them, and re-layouts  17.6 us (13%)
  Pallas kernels  7.62 us (5%)
    ppermute x6, waiting for transfers between devices, shift(): lax.ppermute(x, 'dp', [(i, (i + by) % replicas) for i in range(replicas)])  36.4 us
    all_to_all x2, starting transfers between devices, exchange(): x = lax.all_to_all(x, 'expert', split_axis=0, concat_axis=0, tiled=True)  33.6 us
    ppermute x6, starting transfers between devices, shift(): lax.ppermute(x, 'dp', [(i, (i + by) % replicas) for i in range(replicas)])  20.9 us
    all_to_all x2, waiting for transfers between devices, exchange(): x = lax.all_to_all(x, 'expert', split_axis=0, concat_axis=0, tiled=True)  19 us
    unnamed x28, local copies, waits for them, and re-layouts  6.53 us
    pallas_call x1, Pallas kernels, per_device(): pl.pallas_call(lambda *refs: expert_kernel(model, *refs), out_shape=[jax....  5.82 us
    reshape x2, local copies, waits for them, and re-layouts, exchange(): x = x.reshape(groups, SLOTS, 2 * model)  4.11 us
    reshape x2, local copies, waits for them, and re-layouts, exchange(): return x.reshape(groups * SLOTS, 2 * model)  3.71 us
  transfers between devices with their start and end apart: 8, of which 5 were waited for; matrix products, arithmetic and copies ran while one was open for 4% of the time, Pallas kernels for 0%

profile of v1, /device:TPU:1, one launch (start us, length us, event | category | flops | bytes accessed | tf_op | source)
XLA Modules:
  0.0 136.3 jit_solution(17200688618529791440)
XLA Ops:
  0.6 0.8 copy.11.ids_ref
  1.4 0.8 copy.12.gates_ref
  2.2 0.0 copy-start
  2.2 0.8 copy-done
  3.0 0.8 copy-done.2
  3.7 0.7 dispatch.1
  4.4 1.5 %reshape.40 = bf16[128,2,2048]{2,1,0:T(2,128)(2,1)} reshape(bf16[256,2048]{1,0:T(8,128)(2,1)S(1)} %dispatch.1) | data formatting | bytes 2097152 | tf_op jit(solution)/shard_map/reshape | solution.py:144
  5.9 19.0 %all-to-all-start = ((bf16[128,2,2048]{2,1,0:T(2,128)(2,1)}), bf16[128,2,2048]{2,1,0:T(2,128)(2,1)}, u32[]{:S(2)}, u32[]{:S(2)}) async-start(bf16[128,2,2048]{2,1,0:T(2,128)(2,1)} %reshape.40), calls=%async_computation | async-start | bytes 2097152 | tf_op jit(solution)/shard_map/all_to_all | solution.py:145
  25.0 0.0 copy-done.11
  25.0 0.2 reshape.43
  25.2 0.0 copy-done.10
  25.2 0.1 copy.20
  25.3 0.1 pad_maximum_fusion.refs_1_
  25.4 4.7 %collective-permute-start.2 = (bf16[1536,256]{1,0:T(8,128)(2,1)S(1)}, bf16[1536,256]{1,0:T(8,128)(2,1)S(1)}, u32[]{:S(2)}, u32[]{:S(2)}) collective-permute-start(bf16[1536,256]{1,0:T(8,128)(2,1)S(1)} %pad_maximum_fusion.refs_1_), channel_id=1, source_target_pairs={{0,256},{128,384},{256,0},{384,128},{1,257},{129,385},{257,1},{385... | collective-permute-start | bytes 2359304 | tf_op jit(solution)/shard_map/ppermute | solution.py:124
  30.0 2.2 %collective-permute-start.1 = (bf16[1536,256]{1,0:T(8,128)(2,1)S(1)}, bf16[1536,256]{1,0:T(8,128)(2,1)S(1)}, u32[]{:S(2)}, u32[]{:S(2)}) collective-permute-start(bf16[1536,256]{1,0:T(8,128)(2,1)S(1)} %pad_maximum_fusion.refs_1_), channel_id=1, source_target_pairs={{0,128},{128,256},{256,384},{384,0},{1,129},{129,257},{257,385},{3... | collective-permute-start | bytes 2359304 | tf_op jit(solution)/shard_map/ppermute | solution.py:124
  32.2 4.3 %collective-permute-start = (bf16[1536,256]{1,0:T(8,128)(2,1)S(1)}, bf16[1536,256]{1,0:T(8,128)(2,1)S(1)}, u32[]{:S(2)}, u32[]{:S(2)}) collective-permute-start(bf16[1536,256]{1,0:T(8,128)(2,1)S(1)} %pad_maximum_fusion.refs_1_), channel_id=1, source_target_pairs={{0,384},{128,0},{256,128},{384,256},{1,385},{129,1},{257,129},{385... | collective-permute-start | bytes 2359304 | tf_op jit(solution)/shard_map/ppermute | solution.py:124
  36.5 19.0 %all-to-all-done = bf16[128,2,2048]{2,1,0:T(2,128)(2,1)} async-done(((bf16[128,2,2048]{2,1,0:T(2,128)(2,1)}), bf16[128,2,2048]{2,1,0:T(2,128)(2,1)}, u32[]{:S(2)}, u32[]{:S(2)}) %all-to-all-start) | async-done | bytes 1048608 | tf_op jit(solution)/shard_map/all_to_all | solution.py:145
  55.5 2.2 %reshape.41.refs_0_ = bf16[256,2048]{1,0:T(8,128)(2,1)} reshape(bf16[128,2,2048]{2,1,0:T(2,128)(2,1)} %all-to-all-done) | data formatting | bytes 2097152 | tf_op jit(solution)/shard_map/reshape | solution.py:146
  57.8 0.0 collective-permute-done.2.refs_4_
  57.8 7.3 %collective-permute-done.1.refs_3_ = bf16[1536,256]{1,0:T(8,128)(2,1)S(1)} collective-permute-done((bf16[1536,256]{1,0:T(8,128)(2,1)S(1)}, bf16[1536,256]{1,0:T(8,128)(2,1)S(1)}, u32[]{:S(2)}, u32[]{:S(2)}) %collective-permute-start.1) | collective-permute-done | bytes 786464 | tf_op jit(solution)/shard_map/ppermute | solution.py:124
  65.1 0.0 copy-done.9
  65.1 0.0 collective-permute-done.refs_2_
  65.1 5.8 %expert.1 = (bf16[256,2048]{1,0:T(8,128)(2,1)}, bf16[1536,256]{1,0:T(8,128)(2,1)S(1)}, bf16[1536,256]{1,0:T(8,128)(2,1)S(1)}, bf16[1536,256]{1,0:T(8,128)(2,1)S(1)}, bf16[1536,256]{1,0:T(8,128)(2,1)S(1)}) custom-call(bf16[256,2048]{1,0:T(8,128)(2,1)} %reshape.41.refs_0_, bf16[1536,256]{1,0:T(8,128)(2,1)S(1)} %pad_maximum_fusion.refs_1_, ...), custom_call_target="tpu_custom_call" | custom-call | tf_op jit(solution)/shard_map/expert/pallas_call | solution.py:149
  70.9 0.9 copy-done.3
  71.8 0.9 copy-done.5
  72.7 0.9 copy-done.7
  73.5 2.6 %reshape.45 = bf16[128,2,2048]{2,1,0:T(2,128)(2,1)} reshape(bf16[256,2048]{1,0:T(8,128)(2,1)} %get-tuple-element.13) | data formatting | bytes 2097152 | tf_op jit(solution)/shard_map/reshape | solution.py:144
  76.2 14.6 %all-to-all-start.1 = ((bf16[128,2,2048]{2,1,0:T(2,128)(2,1)}), bf16[128,2,2048]{2,1,0:T(2,128)(2,1)}, u32[]{:S(2)}, u32[]{:S(2)}) async-start(bf16[128,2,2048]{2,1,0:T(2,128)(2,1)} %reshape.45), calls=%async_computation.1 | async-start | bytes 2097152 | tf_op jit(solution)/shard_map/all_to_all | solution.py:145
  90.7 0.0 copy-done.8
  90.7 3.1 %collective-permute-start.3 = (bf16[1536,256]{1,0:T(8,128)(2,1)S(1)}, bf16[1536,256]{1,0:T(8,128)(2,1)S(1)}, u32[]{:S(2)}, u32[]{:S(2)}) collective-permute-start(bf16[1536,256]{1,0:T(8,128)(2,1)S(1)} %copy-done.8), channel_id=1, source_target_pairs={{0,128},{128,256},{256,384},{384,0},{1,129},{129,257},{257,385},{3... | collective-permute-start | bytes 2359304 | tf_op jit(solution)/shard_map/ppermute | solution.py:124
  93.8 0.0 copy-done.6
  93.8 3.4 %collective-permute-start.4 = (bf16[1536,256]{1,0:T(8,128)(2,1)S(1)}, bf16[1536,256]{1,0:T(8,128)(2,1)S(1)}, u32[]{:S(2)}, u32[]{:S(2)}) collective-permute-start(bf16[1536,256]{1,0:T(8,128)(2,1)S(1)} %copy-done.6), channel_id=1, source_target_pairs={{0,384},{128,0},{256,128},{384,256},{1,385},{129,1},{257,129},{385... | collective-permute-start | bytes 2359304 | tf_op jit(solution)/shard_map/ppermute | solution.py:124
  97.3 0.0 copy-done.4
  97.3 3.3 %collective-permute-start.5 = (bf16[1536,256]{1,0:T(8,128)(2,1)S(1)}, bf16[1536,256]{1,0:T(8,128)(2,1)S(1)}, u32[]{:S(2)}, u32[]{:S(2)}) collective-permute-start(bf16[1536,256]{1,0:T(8,128)(2,1)S(1)} %copy-done.4), channel_id=1, source_target_pairs={{0,256},{128,384},{256,0},{384,128},{1,257},{129,385},{257,1},{385... | collective-permute-start | bytes 2359304 | tf_op jit(solution)/shard_map/ppermute | solution.py:124
  100.6 11.4 %collective-permute-done.3 = bf16[1536,256]{1,0:T(8,128)(2,1)S(1)} collective-permute-done((bf16[1536,256]{1,0:T(8,128)(2,1)S(1)}, bf16[1536,256]{1,0:T(8,128)(2,1)S(1)}, u32[]{:S(2)}, u32[]{:S(2)}) %collective-permute-start.3) | collective-permute-done | bytes 786464 | tf_op jit(solution)/shard_map/ppermute | solution.py:124
  112.0 1.6 %collective-permute-done.4 = bf16[1536,256]{1,0:T(8,128)(2,1)S(1)} collective-permute-done((bf16[1536,256]{1,0:T(8,128)(2,1)S(1)}, bf16[1536,256]{1,0:T(8,128)(2,1)S(1)}, u32[]{:S(2)}, u32[]{:S(2)}) %collective-permute-start.4) | collective-permute-done | bytes 786464 | tf_op jit(solution)/shard_map/ppermute | solution.py:124
  113.6 16.0 %collective-permute-done.5 = bf16[1536,256]{1,0:T(8,128)(2,1)S(1)} collective-permute-done((bf16[1536,256]{1,0:T(8,128)(2,1)S(1)}, bf16[1536,256]{1,0:T(8,128)(2,1)S(1)}, u32[]{:S(2)}, u32[]{:S(2)}) %collective-permute-start.5) | collective-permute-done | bytes 786464 | tf_op jit(solution)/shard_map/ppermute | solution.py:124
  129.6 0.4 convert_add_fusion
  130.1 0.1 slice.8
  130.2 1.5 %reshape.47 = f32[1,1024,2,128]{3,2,1,0:T(2,128)} reshape(f32[1024,256]{1,0:T(8,128)S(1)} %slice.8) | data formatting | bytes 2097152 | tf_op jit(solution)/shard_map/reshape | solution.py:170
  131.7 0.3 copy.16
  132.0 0.0 copy-start.1
  132.0 1.1 reshape.49
  133.1 0.0 all-to-all-done.1
  133.1 1.5 %reshape.46.back_ref = bf16[256,2048]{1,0:T(8,128)(2,1)S(1)} reshape(bf16[128,2,2048]{2,1,0:T(2,128)(2,1)} %all-to-all-done.1) | data formatting | bytes 2097152 | tf_op jit(solution)/shard_map/reshape | solution.py:146
  134.6 0.0 copy-done.1
  134.6 1.1 combine.1
  135.7 0.7 copy.17
  (12 shorter events, 0.1 us)
Async XLA Ops:
  2.2 0.8 copy-start
  3.0 0.8 copy-start.2
  5.9 19.0 %copy-start.11 = (bf16[1,128,1024]{2,1,0:T(8,128)(2,1)S(1)}, bf16[1,128,1024]{2,1,0:T(8,128)(2,1)}, u32[]{:S(2)}) copy-start(bf16[1,128,1024]{2,1,0:T(8,128)(2,1)} %param.11) | copy-start | bytes 786436
  5.9 19.3 %copy-start.10 = (bf16[1,1024,2,128]{3,2,1,0:T(2,128)(2,1)S(1)}, bf16[1,1024,2,128]{3,2,1,0:T(2,128)(2,1)}, u32[]{:S(2)}) copy-start(bf16[1,1024,2,128]{3,2,1,0:T(2,128)(2,1)} %param.10) | copy-start | bytes 1572868
  5.9 49.6 %all-to-all-start = ((bf16[128,2,2048]{2,1,0:T(2,128)(2,1)}), bf16[128,2,2048]{2,1,0:T(2,128)(2,1)}, u32[]{:S(2)}, u32[]{:S(2)}) async-start(bf16[128,2,2048]{2,1,0:T(2,128)(2,1)} %reshape.40), calls=%async_computation | async-start | bytes 2097152 | tf_op jit(solution)/shard_map/all_to_all | solution.py:145
  25.4 32.4 %collective-permute-start.2 = (bf16[1536,256]{1,0:T(8,128)(2,1)S(1)}, bf16[1536,256]{1,0:T(8,128)(2,1)S(1)}, u32[]{:S(2)}, u32[]{:S(2)}) collective-permute-start(bf16[1536,256]{1,0:T(8,128)(2,1)S(1)} %pad_maximum_fusion.refs_1_), channel_id=1, source_target_pairs={{0,256},{128,384},{256,0},{384,128},{1,257},{129,385},{257,1},{385... | collective-permute-start | bytes 2359304 | tf_op jit(solution)/shard_map/ppermute | solution.py:124
  30.0 35.1 %collective-permute-start.1 = (bf16[1536,256]{1,0:T(8,128)(2,1)S(1)}, bf16[1536,256]{1,0:T(8,128)(2,1)S(1)}, u32[]{:S(2)}, u32[]{:S(2)}) collective-permute-start(bf16[1536,256]{1,0:T(8,128)(2,1)S(1)} %pad_maximum_fusion.refs_1_), channel_id=1, source_target_pairs={{0,128},{128,256},{256,384},{384,0},{1,129},{129,257},{257,385},{3... | collective-permute-start | bytes 2359304 | tf_op jit(solution)/shard_map/ppermute | solution.py:124
  32.2 32.8 %collective-permute-start = (bf16[1536,256]{1,0:T(8,128)(2,1)S(1)}, bf16[1536,256]{1,0:T(8,128)(2,1)S(1)}, u32[]{:S(2)}, u32[]{:S(2)}) collective-permute-start(bf16[1536,256]{1,0:T(8,128)(2,1)S(1)} %pad_maximum_fusion.refs_1_), channel_id=1, source_target_pairs={{0,384},{128,0},{256,128},{384,256},{1,385},{129,1},{257,129},{385... | collective-permute-start | bytes 2359304 | tf_op jit(solution)/shard_map/ppermute | solution.py:124
  57.8 7.3 %copy-start.9 = (bf16[1536,256]{1,0:T(8,128)(2,1)}, bf16[1536,256]{1,0:T(8,128)(2,1)S(1)}, u32[]{:S(2)}) copy-start(bf16[1536,256]{1,0:T(8,128)(2,1)S(1)} %collective-permute-done.2.refs_4_) | copy-start | bytes 2359300
  70.9 0.9 copy-start.3
  71.8 0.9 copy-start.5
  72.7 0.9 copy-start.7
  73.5 17.2 %copy-start.8 = (bf16[1536,256]{1,0:T(8,128)(2,1)S(1)}, bf16[1536,256]{1,0:T(8,128)(2,1)}, u32[]{:S(2)}) copy-start(bf16[1536,256]{1,0:T(8,128)(2,1)} %copy-done.7) | copy-start | bytes 2359300
  76.2 17.7 %copy-start.6 = (bf16[1536,256]{1,0:T(8,128)(2,1)S(1)}, bf16[1536,256]{1,0:T(8,128)(2,1)}, u32[]{:S(2)}) copy-start(bf16[1536,256]{1,0:T(8,128)(2,1)} %copy-done.5) | copy-start | bytes 2359300
  76.2 21.1 %copy-start.4 = (bf16[1536,256]{1,0:T(8,128)(2,1)S(1)}, bf16[1536,256]{1,0:T(8,128)(2,1)}, u32[]{:S(2)}) copy-start(bf16[1536,256]{1,0:T(8,128)(2,1)} %copy-done.3) | copy-start | bytes 2359300
  76.2 56.9 %all-to-all-start.1 = ((bf16[128,2,2048]{2,1,0:T(2,128)(2,1)}), bf16[128,2,2048]{2,1,0:T(2,128)(2,1)}, u32[]{:S(2)}, u32[]{:S(2)}) async-start(bf16[128,2,2048]{2,1,0:T(2,128)(2,1)} %reshape.45), calls=%async_computation.1 | async-start | bytes 2097152 | tf_op jit(solution)/shard_map/all_to_all | solution.py:145
  90.7 21.3 %collective-permute-start.3 = (bf16[1536,256]{1,0:T(8,128)(2,1)S(1)}, bf16[1536,256]{1,0:T(8,128)(2,1)S(1)}, u32[]{:S(2)}, u32[]{:S(2)}) collective-permute-start(bf16[1536,256]{1,0:T(8,128)(2,1)S(1)} %copy-done.8), channel_id=1, source_target_pairs={{0,128},{128,256},{256,384},{384,0},{1,129},{129,257},{257,385},{3... | collective-permute-start | bytes 2359304 | tf_op jit(solution)/shard_map/ppermute | solution.py:124
  93.8 19.8 %collective-permute-start.4 = (bf16[1536,256]{1,0:T(8,128)(2,1)S(1)}, bf16[1536,256]{1,0:T(8,128)(2,1)S(1)}, u32[]{:S(2)}, u32[]{:S(2)}) collective-permute-start(bf16[1536,256]{1,0:T(8,128)(2,1)S(1)} %copy-done.6), channel_id=1, source_target_pairs={{0,384},{128,0},{256,128},{384,256},{1,385},{129,1},{257,129},{385... | collective-permute-start | bytes 2359304 | tf_op jit(solution)/shard_map/ppermute | solution.py:124
  97.3 32.4 %collective-permute-start.5 = (bf16[1536,256]{1,0:T(8,128)(2,1)S(1)}, bf16[1536,256]{1,0:T(8,128)(2,1)S(1)}, u32[]{:S(2)}, u32[]{:S(2)}) collective-permute-start(bf16[1536,256]{1,0:T(8,128)(2,1)S(1)} %copy-done.4), channel_id=1, source_target_pairs={{0,256},{128,384},{256,0},{384,128},{1,257},{129,385},{257,1},{385... | collective-permute-start | bytes 2359304 | tf_op jit(solution)/shard_map/ppermute | solution.py:124
  132.0 2.6 %copy-start.1 = (bf16[24,1024]{1,0:T(8,128)(2,1)S(1)}, bf16[24,1024]{1,0:T(8,128)(2,1)}, u32[]{:S(2)}) copy-start(bf16[24,1024]{1,0:T(8,128)(2,1)} %grad_ref.3) | copy-start | bytes 147460

commit v2 on v1

v2 whole, which is shorter than its diff:
```python
import jax
import jax.numpy as jnp
from jax import lax
from jax.experimental import pallas as pl
from jax.experimental.pallas import tpu as pltpu
from jax.sharding import PartitionSpec as P

BF16 = jnp.bfloat16
F32 = jnp.float32
SLOTS = 2
PIECE = 8
PEERS = 16
VMEM_LIMIT = 20 * 1024 * 1024
KEEP = int(1.9e10)
BESIDE = int(2e11)
FIRST = (((0,), (0,)), ((), ()))
LAST = (((1,), (1,)), ((), ()))


def routing(ids, gates, groups):
    per_token, count_tok = ids.shape
    slots = groups * SLOTS
    line = lax.broadcasted_iota(jnp.int32, (slots, count_tok), 0)
    expert = line % groups
    place = line // groups
    named = jnp.zeros((slots, count_tok), F32)
    gate = jnp.zeros((slots, count_tok), F32)
    for k in range(per_token):
        hit = ids[k : k + 1, :] == expert
        named = jnp.where(hit, 1.0, named)
        gate = jnp.where(hit, gates[k : k + 1, :], gate)
    row = lax.broadcasted_iota(jnp.int32, (count_tok, count_tok), 0)
    col = lax.broadcasted_iota(jnp.int32, (count_tok, count_tok), 1)
    earlier = (row < col).astype(BF16)
    rank = jnp.dot(named.astype(BF16), earlier, preferred_element_type=F32)
    held = jnp.where(rank == place.astype(F32), named, 0.0)
    return held, held * gate, expert


def three_parts(x):
    high = x.astype(BF16)
    rest = x - high.astype(F32)
    mid = rest.astype(BF16)
    low = (rest - mid.astype(F32)).astype(BF16)
    return high, mid, low


def weave(back):
    size = PEERS * PIECE
    major, minor = (PIECE, PEERS) if back else (PEERS, PIECE)
    row = lax.broadcasted_iota(jnp.int32, (size, size), 0)
    col = lax.broadcasted_iota(jnp.int32, (size, size), 1)
    return ((row % minor) * major + row // minor == col).astype(BF16)


def weave_blocks(first, second, wire_ref):
    groups = first.shape[0] // SLOTS
    half = first.shape[1] // 2
    size = PEERS * PIECE
    permute = weave(False)
    for b in range(groups // PEERS):
        parts = []
        for array in (first, second):
            for c in range(SLOTS):
                lines = array[c * groups + b * PEERS : c * groups + (b + 1) * PEERS]
                parts += [lines[:, :half], lines[:, half:]]
        wire_ref[b * size : (b + 1) * size, :] = jnp.dot(
            permute, jnp.concatenate(parts, axis=0), preferred_element_type=F32
        ).astype(BF16)


def unweave_blocks(wire_ref, first_ref, second_ref):
    groups = first_ref.shape[0] // SLOTS
    half = first_ref.shape[1] // 2
    size = PEERS * PIECE
    permute = weave(True)
    for b in range(groups // PEERS):
        lines = jnp.dot(
            permute, wire_ref[b * size : (b + 1) * size, :], preferred_element_type=F32
        ).astype(BF16)
        i = 0
        for ref in (first_ref, second_ref):
            for c in range(SLOTS):
                for h in range(2):
                    ref[c * groups + b * PEERS : c * groups + (b + 1) * PEERS, h * half : (h + 1) * half] = lines[
                        i * PEERS : (i + 1) * PEERS
                    ]
                    i += 1


def start_all(pairs, sem):
    copies = [pltpu.make_async_copy(source, target, sem.at[i]) for i, (source, target) in enumerate(pairs)]
    for copy in copies:
        copy.start()
    return copies


def wait_all(copies):
    for copy in copies:
        copy.wait()


def dispatch_kernel(
    in_hbm, out_hbm, tokens_hbm, grad_hbm, ids_hbm, gates_hbm, packed_hbm, send_hbm,
    raw_ref, packed_ref, tokens_ref, grad_ref, ids_ref, gates_ref, wire_ref, sem, wire_sem,
):
    model = in_hbm.shape[0]
    groups = send_hbm.shape[0] // PIECE
    wide = packed_ref.shape[1]
    width = wide // 2
    pairs = [(ids_hbm, ids_ref), (gates_hbm, gates_ref), (in_hbm, raw_ref)]
    for i in range(model // wide):
        pairs.append(
            (
                out_hbm.at[:, i * wide : (i + 1) * wide],
                packed_ref.at[model + i * width : model + (i + 1) * width, :],
            )
        )
    pairs += [(tokens_hbm, tokens_ref), (grad_hbm, grad_ref)]
    copies = start_all(pairs, sem)
    copies[0].wait()
    copies[1].wait()
    held, gate, _ = routing(ids_ref[...], gates_ref[...], groups)
    wait_all(copies[2:-2])
    raw = raw_ref[...]
    packed_ref[:model, :width] = raw[:, 0, :]
    packed_ref[:model, width:] = raw[:, 1, :]
    leaving = pltpu.make_async_copy(packed_ref, packed_hbm, sem.at[0])
    leaving.start()
    wait_all(copies[-2:])
    rows = jnp.dot(held.astype(BF16), tokens_ref[...], preferred_element_type=F32).astype(BF16)
    grad = grad_ref[...]
    grad_rows = jnp.dot(
        jnp.concatenate(three_parts(gate), axis=1),
        jnp.concatenate([grad, grad, grad], axis=0),
        preferred_element_type=F32,
    ).astype(BF16)
    weave_blocks(rows, grad_rows, wire_ref)
    sending = pltpu.make_async_copy(wire_ref, send_hbm, wire_sem)
    sending.start()
    leaving.wait()
    sending.wait()


def assembly(sources, in_ref, out_ref):
    model = in_ref.shape[0]
    wide = sources[0].shape[1]
    width = wide // 2
    pairs = []
    for r, source in enumerate(sources):
        pairs.append((source.at[:model, :], in_ref.at[:, r * wide : (r + 1) * wide]))
        for i in range(model // wide):
            pairs.append(
                (
                    source.at[model + i * width : model + (i + 1) * width, :],
                    out_ref.at[r * width : (r + 1) * width, i * wide : (i + 1) * wide],
                )
            )
    return pairs


def weight_grads(rows, grad_rows, hidden, grad_pre, r, grad_ref):
    model = rows.shape[1]
    wide = grad_ref.shape[1]
    width = wide // 2
    grad_ref[:model, :] = lax.dot_general(
        rows, grad_pre[:, r * wide : (r + 1) * wide], FIRST, preferred_element_type=F32
    ).astype(BF16)
    value = lax.dot_general(
        hidden[:, r * width : (r + 1) * width], grad_rows, FIRST, preferred_element_type=F32
    ).astype(BF16)
    for i in range(model // wide):
        grad_ref[model + i * width : model + (i + 1) * width, :] = value[:, i * wide : (i + 1) * wide]


def expert_kernel(
    pieces, wire_hbm, *refs
):
    sources, back_hbm, grads_hbm = refs[:pieces], refs[pieces], refs[pieces + 1 : 2 * pieces + 1]
    grads = refs[2 * pieces + 1 : 3 * pieces + 1]
    (
        in_ref, out_ref, wire_ref, rows_ref, grad_rows_ref, hidden_ref, grad_pre_ref, sem, weights_sem, grad_sem
    ) = refs[3 * pieces + 1 :]
    wide = grads[0].shape[1]
    width = wide // 2
    arriving = pltpu.make_async_copy(wire_hbm, wire_ref, sem)
    arriving.start()
    weights = start_all(assembly(sources, in_ref, out_ref), weights_sem)
    arriving.wait()
    unweave_blocks(wire_ref, rows_ref, grad_rows_ref)
    wait_all(weights)
    rows = rows_ref[...]
    grad_rows = grad_rows_ref[...]
    preact = jnp.dot(rows, in_ref[...], preferred_element_type=F32)
    back = lax.dot_general(grad_rows, out_ref[...], LAST, preferred_element_type=F32)
    for r in range(pieces):
        gate_part = preact[:, r * wide : r * wide + width]
        up_part = preact[:, r * wide + width : (r + 1) * wide]
        back_part = back[:, r * width : (r + 1) * width]
        sig = jax.nn.sigmoid(gate_part)
        activated = gate_part * sig
        grad_gate = back_part * up_part * (sig * (1.0 + gate_part * (1.0 - sig)))
        hidden_ref[:, r * width : (r + 1) * width] = (activated * up_part).astype(BF16)
        grad_pre_ref[:, r * wide : r * wide + width] = grad_gate.astype(BF16)
        grad_pre_ref[:, r * wide + width : (r + 1) * wide] = (back_part * activated).astype(BF16)
    hidden = hidden_ref[...]
    grad_pre = grad_pre_ref[...]
    result = jnp.dot(hidden, out_ref[...], preferred_element_type=F32).astype(BF16)
    dx = lax.dot_general(grad_pre, in_ref[...], LAST, preferred_element_type=F32).astype(BF16)
    weave_blocks(result, dx, wire_ref)
    sending = pltpu.make_async_copy(wire_ref, back_hbm, sem)
    sending.start()
    order = (1, 2, 3, 0)
    for r in order:
        weight_grads(rows, grad_rows, hidden, grad_pre, r, grads[r])
    leaving = start_all([(grads[r], grads_hbm[r]) for r in order], grad_sem)
    sending.wait()
    wait_all(leaving)


def finish_kernel(
    wire_hbm, grad_hbm, ids_hbm, gates_hbm, partial_any, next_any, last_any,
    mixed_ref, dx_ref, gate_grad_ref, in_hbm, out_hbm,
    wire_ref, result_ref, back_ref, grad_ref, ids_ref, gates_ref,
    partial_ref, next_ref, last_ref, in_ref, out_ref, sem, out_sem,
):
    groups = result_ref.shape[0] // SLOTS
    model = result_ref.shape[1]
    wide = next_ref.shape[1]
    width = wide // 2
    copies = start_all(
        [(ids_hbm, ids_ref), (gates_hbm, gates_ref), (partial_any, partial_ref), (next_any, next_ref)]
        + [(last_any, last_ref), (grad_hbm, grad_ref), (wire_hbm, wire_ref)],
        sem,
    )
    wait_all(copies[:2])
    ids = ids_ref[...]
    per_token, count_tok = ids.shape
    held, gate, expert = routing(ids, gates_ref[...], groups)
    mix = jnp.concatenate([part.astype(F32) for part in three_parts(gate)] + [held], axis=1).T.astype(BF16)

    def total(lower, size):
        value = partial_ref[lower : lower + size, :]
        for piece in (next_ref, last_ref):
            value = value + piece[lower : lower + size, :].astype(F32)
        return value

    wait_all(copies[2:])
    value = total(0, model)
    in_ref[pl.ds(0, model, stride=2), :] = value[:, :width]
    in_ref[pl.ds(1, model, stride=2), :] = value[:, width:]
    for i in range(model // wide):
        out_ref[:, i * wide : (i + 1) * wide] = total(model + i * width, width)
    leaving = start_all([(in_ref, in_hbm), (out_ref, out_hbm)], out_sem)
    unweave_blocks(wire_ref, result_ref, back_ref)
    result = result_ref[...]
    gate_rows = 3 * count_tok
    mixed = jnp.dot(mix[:gate_rows], result, preferred_element_type=F32)
    mixed_ref[...] = (
        mixed[:count_tok] + mixed[count_tok : 2 * count_tok] + mixed[2 * count_tok :]
    ).astype(BF16)
    dx_ref[...] = jnp.dot(mix[gate_rows:], back_ref[...], preferred_element_type=F32).astype(BF16)
    inner = lax.dot_general(result, grad_ref[...], LAST, preferred_element_type=F32) * held
    for k in range(per_token):
        hit = ids[k : k + 1, :] == expert
        gate_grad_ref[k : k + 1, :] = jnp.sum(jnp.where(hit, inner, 0.0), axis=0, keepdims=True)
    wait_all(leaving)


def add_kernel(first_ref, second_ref, total_ref):
    total_ref[...] = first_ref[...].astype(F32) + second_ref[...].astype(F32)


def per_device(tokens, grad_out, expert_ids, gates, w_in, w_out):
    count_tok, model = tokens.shape
    per_token = gates.shape[1]
    groups = lax.axis_size("expert")
    replicas = lax.axis_size("dp")
    width = w_out.shape[1]
    wide = 2 * width
    slots = groups * SLOTS
    wire = jax.ShapeDtypeStruct((groups * PIECE, model // 2), BF16)
    params = pltpu.CompilerParams(vmem_limit_bytes=VMEM_LIMIT)
    in_hbm = pl.BlockSpec(memory_space=pltpu.HBM)
    anywhere = pl.BlockSpec(memory_space=pl.ANY)
    in_vmem = pl.BlockSpec(memory_space=pltpu.VMEM)
    small = pltpu.CompilerParams(vmem_limit_bytes=4 * 1024 * 1024)

    def shift(x, by):
        return lax.ppermute(x, "dp", [(i, (i + by) % replicas) for i in range(replicas)])

    def held_in(x, space):
        return pltpu.with_memory_space_constraint(x, space)

    def exchange(x):
        x = x.reshape(groups, PIECE, model // 2)
        x = lax.all_to_all(x, "expert", split_axis=0, concat_axis=0, tiled=True)
        return x.reshape(groups * PIECE, model // 2)

    ids_t, gates_t = expert_ids.T, gates.T
    tokens_like = pltpu.VMEM(tokens.shape, BF16)
    ids_like = pltpu.VMEM(ids_t.shape, jnp.int32)
    gates_like = pltpu.VMEM(gates_t.shape, F32)
    piece = (model + width * (model // wide), wide)
    piece_like = pltpu.VMEM(piece, BF16)
    rows_like = pltpu.VMEM((slots, model), BF16)
    hidden_like = pltpu.VMEM((slots, replicas * width), BF16)
    grad_pre_like = pltpu.VMEM((slots, replicas * wide), BF16)
    wire_like = pltpu.VMEM(wire.shape, BF16)
    lines = 1 + model // wide
    inputs = [w_in.reshape(model, 2, width), w_out.reshape(width, model), tokens, grad_out, ids_t, gates_t]
    packed, send = pl.pallas_call(
        dispatch_kernel,
        out_shape=[pltpu.HBM(piece, BF16), pltpu.HBM(wire.shape, BF16)],
        in_specs=[in_hbm] * 6,
        out_specs=[in_hbm] * 2,
        scratch_shapes=[
            pltpu.VMEM((model, 2, width), BF16),
            piece_like, tokens_like, tokens_like, ids_like, gates_like, wire_like,
            pltpu.SemaphoreType.DMA((lines + 4,)),
            pltpu.SemaphoreType.DMA,
        ],
        compiler_params=params,
        name="dispatch",
    )(*[held_in(x, pltpu.HBM) for x in inputs])
    far = shift(packed, -2)
    far_late = pl.pallas_call(
        lambda far_hbm, out_ref, sem: wait_all(start_all([(far_hbm, out_ref)], sem)),
        out_shape=piece_like,
        in_specs=[anywhere],
        scratch_shapes=[pltpu.SemaphoreType.DMA((1,))],
        compiler_params=small,
        cost_estimate=pl.CostEstimate(flops=KEEP, bytes_accessed=0, transcendentals=0),
        name="keep",
    )(far)
    arrived = exchange(send)

    back, own, grad_far, grad_next, grad_last = pl.pallas_call(
        lambda *refs: expert_kernel(replicas, *refs),
        out_shape=[pltpu.HBM(wire.shape, BF16)] + [pltpu.HBM(piece, BF16)] * replicas,
        in_specs=[in_hbm] + [anywhere] * replicas,
        out_specs=[in_hbm] * (1 + replicas),
        scratch_shapes=[piece_like] * replicas
        + [
            pltpu.VMEM((model, replicas * wide), BF16),
            pltpu.VMEM((replicas * width, model), BF16),
            wire_like, rows_like, rows_like, hidden_like, grad_pre_like,
            pltpu.SemaphoreType.DMA,
            pltpu.SemaphoreType.DMA((replicas * lines,)),
            pltpu.SemaphoreType.DMA((replicas,)),
        ],
        compiler_params=params,
        name="expert",
    )(arrived, held_in(packed, pltpu.HBM), far_late, shift(packed, -1), shift(packed, 1))
    returned = exchange(back)
    partial = pl.pallas_call(
        add_kernel,
        out_shape=jax.ShapeDtypeStruct(piece, F32),
        compiler_params=params,
        cost_estimate=pl.CostEstimate(flops=BESIDE, bytes_accessed=0, transcendentals=0),
        name="add",
    )(own, shift(grad_far, 2))
    mixed, grad_tokens, gate_grad, sum_in, sum_out = pl.pallas_call(
        finish_kernel,
        out_shape=[
            jax.ShapeDtypeStruct(tokens.shape, BF16),
            jax.ShapeDtypeStruct(tokens.shape, BF16),
            jax.ShapeDtypeStruct((per_token, count_tok), F32),
            pltpu.HBM((2 * model, width), F32),
            pltpu.HBM((width, model), F32),
        ],
        in_specs=[in_hbm] * 4 + [anywhere] * 3,
        out_specs=[in_vmem] * 3 + [in_hbm] * 2,
        scratch_shapes=[
            wire_like, rows_like, rows_like, tokens_like, ids_like, gates_like,
            pltpu.VMEM(piece, F32), piece_like, piece_like,
            pltpu.VMEM((2 * model, width), F32),
            pltpu.VMEM((width, model), F32),
            pltpu.SemaphoreType.DMA((7,)),
            pltpu.SemaphoreType.DMA((2,)),
        ],
        compiler_params=params,
        name="finish",
    )(
        returned, *[held_in(x, pltpu.HBM) for x in (grad_out, ids_t, gates_t)],
        partial, shift(grad_next, 1), shift(grad_last, -1),
    )
    return mixed, grad_tokens, gate_grad.T, sum_in.reshape(1, model, 2, width), sum_out[None]


def solution(mesh):
    in_specs = (
        P(("dp", "expert"), None),
        P(("dp", "expert"), None),
        P(("dp", "expert"), None),
        P(("dp", "expert"), None),
        P("expert", None, None, "dp"),
        P("expert", "dp", None),
    )
    out_specs = (
        P(("dp", "expert"), None),
        P(("dp", "expert"), None),
        P(("dp", "expert"), None),
        P("expert", None, None, "dp"),
        P("expert", "dp", None),
    )
    return jax.shard_map(
        per_device, mesh=mesh, in_specs=in_specs, out_specs=out_specs, check_vma=False
    )
```

time: 139 us -> 113 us (0.81); the launches traced: 136 us -> 112 us
  local copies, waits for them, and re-layouts: 17.6 us -> 2.05 us
  waiting for transfers between devices: 55.3 us -> 46.1 us
  Pallas kernels: 7.62 us -> 15 us
  starting transfers between devices: 54.5 us -> 48 us
    reshape x8 -> x0, local copies, waits for them, and re-layouts: 10.6 us -> none  [the longest x2 4.11 us: exchange(): x = x.reshape(groups, SLOTS, 2 * model)]
    all_to_all x2, waiting for transfers between devices: 19 us -> 10.5 us  [exchange(): x = lax.all_to_all(x, 'expert', split_axis=0, concat_axis=0, tiled=True)]
    pallas_call x3 -> x5, Pallas kernels: 7.62 us -> 15 us  [the longest x1 5.73 us: per_device(): pl.pallas_call(lambda *refs: expert_kernel(replicas, *refs), out_shape=[p...]
    all_to_all x2, starting transfers between devices: 33.6 us -> 27.3 us  [exchange(): x = lax.all_to_all(x, 'expert', split_axis=0, concat_axis=0, tiled=True)]
    unnamed x28 -> x6, local copies, waits for them, and re-layouts: 6.53 us -> 2.05 us
  transfers between devices with their start and end apart: 8 -> 8, of which waited for: 5 -> 6; matrix products, arithmetic and copies ran while one was open for 4% -> 0% of each run, Pallas kernels for 0% -> 0%
where the time goes in v2:
time: 113 us; the launch traced here: 112 us
  starting transfers between devices  48 us (42%)
  waiting for transfers between devices  46.1 us (41%)
  Pallas kernels  15 us (13%)
  local copies, waits for them, and re-layouts  2.05 us (2%)
    ppermute x6, waiting for transfers between devices, shift(): lax.ppermute(x, 'dp', [(i, (i + by) % replicas) for i in range(replicas)])  35.6 us
    all_to_all x2, starting transfers between devices, exchange(): x = lax.all_to_all(x, 'expert', split_axis=0, concat_axis=0, tiled=True)  27.3 us
    ppermute x6, starting transfers between devices, shift(): lax.ppermute(x, 'dp', [(i, (i + by) % replicas) for i in range(replicas)])  20.7 us
    all_to_all x2, waiting for transfers between devices, exchange(): x = lax.all_to_all(x, 'expert', split_axis=0, concat_axis=0, tiled=True)  10.5 us
    pallas_call x1, Pallas kernels, per_device(): pl.pallas_call(lambda *refs: expert_kernel(replicas, *refs), out_shape=[p...  5.73 us
    pallas_call x1, Pallas kernels, per_device(): pl.pallas_call(finish_kernel, out_shape=[jax.ShapeDtypeStruct(tokens.shap...  4.89 us
    pallas_call x1, Pallas kernels, per_device(): pl.pallas_call(dispatch_kernel, out_shape=[pltpu.HBM(piece, BF16), pltpu....  4.14 us
  transfers between devices with their start and end apart: 8, of which 6 were waited for; matrix products, arithmetic and copies ran while one was open for 0% of the time, Pallas kernels for 0%

profile of v2, /device:TPU:1, one launch (start us, length us, event | category | flops | bytes accessed | tf_op | source)
XLA Modules:
  0.0 111.9 jit_solution(4956311176256893175)
XLA Ops:
  0.6 4.1 %dispatch.1 = (bf16[1536,256]{1,0:T(8,128)(2,1)}, bf16[1024,512]{1,0:T(8,128)(2,1)}) custom-call(bf16[1024,2,128]{2,1,0:T(2,128)(2,1)} %bitcast.14, bf16[128,1024]{1,0:T(8,128)(2,1)} %bitcast.15, bf16[24,1024]{1,0:T(8,128)(2,1)} %tokens_hbm.1, bf16[24,1024]{1,0:T(8,128)(2,1)} %grad_hbm.3, s32[8,24]{1,0:T(8,128)} %bitcast.16, f32[8,24]{1,0:T(8,128)} %bitcast.18), custom_call_target="tpu_custom_call" | custom-call | tf_op jit(solution)/shard_map/dispatch/pallas_call | solution.py:312
  4.8 5.5 %collective-permute-start = (bf16[1536,256]{1,0:T(8,128)(2,1)}, bf16[1536,256]{1,0:T(8,128)(2,1)S(1)}, u32[]{:S(2)}, u32[]{:S(2)}) collective-permute-start(bf16[1536,256]{1,0:T(8,128)(2,1)} %get-tuple-element.18.refs_1_), channel_id=1, source_target_pairs={{0,256},{128,384},{256,0},{384,128},{1,257},{129,385},{257,1},{385... | collective-permute-start | bytes 2359304 | tf_op jit(solution)/shard_map/ppermute | solution.py:290
  10.3 17.9 %all-to-all-start = ((bf16[128,8,512]{2,1,0:T(8,128)(2,1)}), bf16[128,8,512]{2,1,0:T(8,128)(2,1)S(1)}, u32[]{:S(2)}, u32[]{:S(2)}) async-start(bf16[128,8,512]{2,1,0:T(8,128)(2,1)} %bitcast.13), calls=%async_computation | async-start | bytes 2097152 | tf_op jit(solution)/shard_map/all_to_all | solution.py:297
  28.2 2.2 %collective-permute-start.2 = (bf16[1536,256]{1,0:T(8,128)(2,1)}, bf16[1536,256]{1,0:T(8,128)(2,1)S(1)}, u32[]{:S(2)}, u32[]{:S(2)}) collective-permute-start(bf16[1536,256]{1,0:T(8,128)(2,1)} %get-tuple-element.18.refs_1_), channel_id=1, source_target_pairs={{0,128},{128,256},{256,384},{384,0},{1,129},{129,257},{257,385},{3... | collective-permute-start | bytes 2359304 | tf_op jit(solution)/shard_map/ppermute | solution.py:290
  30.4 4.3 %collective-permute-start.1 = (bf16[1536,256]{1,0:T(8,128)(2,1)}, bf16[1536,256]{1,0:T(8,128)(2,1)S(1)}, u32[]{:S(2)}, u32[]{:S(2)}) collective-permute-start(bf16[1536,256]{1,0:T(8,128)(2,1)} %get-tuple-element.18.refs_1_), channel_id=1, source_target_pairs={{0,384},{128,0},{256,128},{384,256},{1,385},{129,1},{257,129},{385... | collective-permute-start | bytes 2359304 | tf_op jit(solution)/shard_map/ppermute | solution.py:290
  34.7 0.0 collective-permute-done.far_hbm
  34.7 0.0 copy-start.1
  34.7 0.9 copy-done.1
  35.6 0.0 copy-start.2
  35.6 1.1 %copy-done.2 = bf16[1536,256]{1,0:T(8,128)(2,1)S(1)} copy-done((bf16[1536,256]{1,0:T(8,128)(2,1)S(1)}, bf16[1536,256]{1,0:T(8,128)(2,1)}, u32[]{:S(2)}) %copy-start.2) | copy-done | bytes 786456
  36.7 0.1 keep.1.refs_2_
  36.8 12.8 %collective-permute-done.2.refs_4_ = bf16[1536,256]{1,0:T(8,128)(2,1)S(1)} collective-permute-done((bf16[1536,256]{1,0:T(8,128)(2,1)}, bf16[1536,256]{1,0:T(8,128)(2,1)S(1)}, u32[]{:S(2)}, u32[]{:S(2)}) %collective-permute-start.2) | collective-permute-done | bytes 786464 | tf_op jit(solution)/shard_map/ppermute | solution.py:290
  49.6 1.0 collective-permute-done.1.refs_3_
  50.6 8.4 %all-to-all-done = bf16[128,8,512]{2,1,0:T(8,128)(2,1)S(1)} async-done(((bf16[128,8,512]{2,1,0:T(8,128)(2,1)}), bf16[128,8,512]{2,1,0:T(8,128)(2,1)S(1)}, u32[]{:S(2)}, u32[]{:S(2)}) %all-to-all-start) | async-done | bytes 1048608 | tf_op jit(solution)/shard_map/all_to_all | solution.py:297
  59.1 5.7 %expert.1 = (bf16[1024,512]{1,0:T(8,128)(2,1)}, bf16[1536,256]{1,0:T(8,128)(2,1)}, bf16[1536,256]{1,0:T(8,128)(2,1)}, bf16[1536,256]{1,0:T(8,128)(2,1)}, bf16[1536,256]{1,0:T(8,128)(2,1)}) custom-call(bf16[1024,512]{1,0:T(8,128)(2,1)S(1)} %bitcast.11, bf16[1536,256]{1,0:T(8,128)(2,1)} %get-tuple-element.18.refs_1_, bf16[1536,256]{1,0:T(8,128)(2,1)S(1)} %keep.1.refs_2_, ...), custom_call_target="tpu_custom_call" | custom-call | tf_op jit(solution)/shard_map/expert/pallas_call | solution.py:338
  64.8 0.0 copy-start
  64.8 2.3 %collective-permute-start.3 = (bf16[1536,256]{1,0:T(8,128)(2,1)}, bf16[1536,256]{1,0:T(8,128)(2,1)S(1)}, u32[]{:S(2)}, u32[]{:S(2)}) collective-permute-start(bf16[1536,256]{1,0:T(8,128)(2,1)} %get-tuple-element.21), channel_id=1, source_target_pairs={{0,256},{128,384},{256,0},{384,128},{1,257},{129,385},{257,1},{385... | collective-permute-start | bytes 2359304 | tf_op jit(solution)/shard_map/ppermute | solution.py:290
  67.1 9.4 %all-to-all-start.1 = ((bf16[128,8,512]{2,1,0:T(8,128)(2,1)}), bf16[128,8,512]{2,1,0:T(8,128)(2,1)}, u32[]{:S(2)}, u32[]{:S(2)}) async-start(bf16[128,8,512]{2,1,0:T(8,128)(2,1)} %bitcast.12), calls=%async_computation.1 | async-start | bytes 2097152 | tf_op jit(solution)/shard_map/all_to_all | solution.py:297
  76.5 4.0 %collective-permute-start.4 = (bf16[1536,256]{1,0:T(8,128)(2,1)}, bf16[1536,256]{1,0:T(8,128)(2,1)}, u32[]{:S(2)}, u32[]{:S(2)}) collective-permute-start(bf16[1536,256]{1,0:T(8,128)(2,1)} %get-tuple-element.22), channel_id=1, source_target_pairs={{0,128},{128,256},{256,384},{384,0},{1,129},{129,257},{257,385},{3... | collective-permute-start | bytes 2359304 | tf_op jit(solution)/shard_map/ppermute | solution.py:290
  80.4 2.5 %collective-permute-start.5 = (bf16[1536,256]{1,0:T(8,128)(2,1)}, bf16[1536,256]{1,0:T(8,128)(2,1)}, u32[]{:S(2)}, u32[]{:S(2)}) collective-permute-start(bf16[1536,256]{1,0:T(8,128)(2,1)} %get-tuple-element.23), channel_id=1, source_target_pairs={{0,384},{128,0},{256,128},{384,256},{1,385},{129,1},{257,129},{385... | collective-permute-start | bytes 2359304 | tf_op jit(solution)/shard_map/ppermute | solution.py:290
  83.0 4.6 %collective-permute-done.3.second_ref = bf16[1536,256]{1,0:T(8,128)(2,1)S(1)} collective-permute-done((bf16[1536,256]{1,0:T(8,128)(2,1)}, bf16[1536,256]{1,0:T(8,128)(2,1)S(1)}, u32[]{:S(2)}, u32[]{:S(2)}) %collective-permute-start.3) | collective-permute-done | bytes 786464 | tf_op jit(solution)/shard_map/ppermute | solution.py:290
  87.5 0.0 copy-done
  87.5 0.2 add.1.partial_any
  87.7 17.3 %collective-permute-done.4.next_any = bf16[1536,256]{1,0:T(8,128)(2,1)} collective-permute-done((bf16[1536,256]{1,0:T(8,128)(2,1)}, bf16[1536,256]{1,0:T(8,128)(2,1)}, u32[]{:S(2)}, u32[]{:S(2)}) %collective-permute-start.4) | collective-permute-done | bytes 786464 | tf_op jit(solution)/shard_map/ppermute | solution.py:290
  105.0 0.0 collective-permute-done.5.last_any
  105.0 2.0 %all-to-all-done.1 = bf16[128,8,512]{2,1,0:T(8,128)(2,1)} async-done(((bf16[128,8,512]{2,1,0:T(8,128)(2,1)}), bf16[128,8,512]{2,1,0:T(8,128)(2,1)}, u32[]{:S(2)}, u32[]{:S(2)}) %all-to-all-start.1) | async-done | bytes 1048608 | tf_op jit(solution)/shard_map/all_to_all | solution.py:297
  107.0 4.9 %finish.1 = (bf16[24,1024]{1,0:T(8,128)(2,1)}, bf16[24,1024]{1,0:T(8,128)(2,1)}, f32[8,24]{1,0:T(8,128)}, f32[2048,128]{1,0:T(8,128)}, f32[128,1024]{1,0:T(8,128)}) custom-call(bf16[1024,512]{1,0:T(8,128)(2,1)} %bitcast.7.wire_hbm, bf16[24,1024]{1,0:T(8,128)(2,1)} %grad_hbm.3, s32[8,24]{1,0:T(8,128)} %bitcast.17, f32[8,24]{1,0:T(8,128)} %bitcast.19, ...), custom_call_target="tpu_custom_call" | custom-call | tf_op jit(solution)/shard_map/finish/pallas_call | solution.py:363
Async XLA Ops:
  4.8 29.9 %collective-permute-start = (bf16[1536,256]{1,0:T(8,128)(2,1)}, bf16[1536,256]{1,0:T(8,128)(2,1)S(1)}, u32[]{:S(2)}, u32[]{:S(2)}) collective-permute-start(bf16[1536,256]{1,0:T(8,128)(2,1)} %get-tuple-element.18.refs_1_), channel_id=1, source_target_pairs={{0,256},{128,384},{256,0},{384,128},{1,257},{129,385},{257,1},{385... | collective-permute-start | bytes 2359304 | tf_op jit(solution)/shard_map/ppermute | solution.py:290
  10.3 48.8 %all-to-all-start = ((bf16[128,8,512]{2,1,0:T(8,128)(2,1)}), bf16[128,8,512]{2,1,0:T(8,128)(2,1)S(1)}, u32[]{:S(2)}, u32[]{:S(2)}) async-start(bf16[128,8,512]{2,1,0:T(8,128)(2,1)} %bitcast.13), calls=%async_computation | async-start | bytes 2097152 | tf_op jit(solution)/shard_map/all_to_all | solution.py:297
  28.2 21.5 %collective-permute-start.2 = (bf16[1536,256]{1,0:T(8,128)(2,1)}, bf16[1536,256]{1,0:T(8,128)(2,1)S(1)}, u32[]{:S(2)}, u32[]{:S(2)}) collective-permute-start(bf16[1536,256]{1,0:T(8,128)(2,1)} %get-tuple-element.18.refs_1_), channel_id=1, source_target_pairs={{0,128},{128,256},{256,384},{384,0},{1,129},{129,257},{257,385},{3... | collective-permute-start | bytes 2359304 | tf_op jit(solution)/shard_map/ppermute | solution.py:290
  30.4 20.2 %collective-permute-start.1 = (bf16[1536,256]{1,0:T(8,128)(2,1)}, bf16[1536,256]{1,0:T(8,128)(2,1)S(1)}, u32[]{:S(2)}, u32[]{:S(2)}) collective-permute-start(bf16[1536,256]{1,0:T(8,128)(2,1)} %get-tuple-element.18.refs_1_), channel_id=1, source_target_pairs={{0,384},{128,0},{256,128},{384,256},{1,385},{129,1},{257,129},{385... | collective-permute-start | bytes 2359304 | tf_op jit(solution)/shard_map/ppermute | solution.py:290
  34.7 0.9 copy-start.1
  35.6 1.1 %copy-start.2 = (bf16[1536,256]{1,0:T(8,128)(2,1)S(1)}, bf16[1536,256]{1,0:T(8,128)(2,1)}, u32[]{:S(2)}) copy-start(bf16[1536,256]{1,0:T(8,128)(2,1)} %copy-done.1) | copy-start | bytes 2359300
  64.8 22.7 %copy-start = (bf16[1536,256]{1,0:T(8,128)(2,1)S(1)}, bf16[1536,256]{1,0:T(8,128)(2,1)}, u32[]{:S(2)}) copy-start(bf16[1536,256]{1,0:T(8,128)(2,1)} %get-tuple-element.20.first_ref) | copy-start | bytes 2359300
  64.8 22.7 %collective-permute-start.3 = (bf16[1536,256]{1,0:T(8,128)(2,1)}, bf16[1536,256]{1,0:T(8,128)(2,1)S(1)}, u32[]{:S(2)}, u32[]{:S(2)}) collective-permute-start(bf16[1536,256]{1,0:T(8,128)(2,1)} %get-tuple-element.21), channel_id=1, source_target_pairs={{0,256},{128,384},{256,0},{384,128},{1,257},{129,385},{257,1},{385... | collective-permute-start | bytes 2359304 | tf_op jit(solution)/shard_map/ppermute | solution.py:290
  67.1 39.9 %all-to-all-start.1 = ((bf16[128,8,512]{2,1,0:T(8,128)(2,1)}), bf16[128,8,512]{2,1,0:T(8,128)(2,1)}, u32[]{:S(2)}, u32[]{:S(2)}) async-start(bf16[128,8,512]{2,1,0:T(8,128)(2,1)} %bitcast.12), calls=%async_computation.1 | async-start | bytes 2097152 | tf_op jit(solution)/shard_map/all_to_all | solution.py:297
  76.5 28.5 %collective-permute-start.4 = (bf16[1536,256]{1,0:T(8,128)(2,1)}, bf16[1536,256]{1,0:T(8,128)(2,1)}, u32[]{:S(2)}, u32[]{:S(2)}) collective-permute-start(bf16[1536,256]{1,0:T(8,128)(2,1)} %get-tuple-element.22), channel_id=1, source_target_pairs={{0,128},{128,256},{256,384},{384,0},{1,129},{129,257},{257,385},{3... | collective-permute-start | bytes 2359304 | tf_op jit(solution)/shard_map/ppermute | solution.py:290
  80.4 24.5 %collective-permute-start.5 = (bf16[1536,256]{1,0:T(8,128)(2,1)}, bf16[1536,256]{1,0:T(8,128)(2,1)}, u32[]{:S(2)}, u32[]{:S(2)}) collective-permute-start(bf16[1536,256]{1,0:T(8,128)(2,1)} %get-tuple-element.23), channel_id=1, source_target_pairs={{0,384},{128,0},{256,128},{384,256},{1,385},{129,1},{257,129},{385... | collective-permute-start | bytes 2359304 | tf_op jit(solution)/shard_map/ppermute | solution.py:290

commit v3 on v2

--- a/solution.py
+++ b/solution.py
@@ -10,9 +10,9 @@
 SLOTS = 2
 PIECE = 8
 PEERS = 16
-VMEM_LIMIT = 20 * 1024 * 1024
+MIB = 1024 * 1024
 KEEP = int(1.9e10)
-BESIDE = int(2e11)
+BESIDE = int(1e11)
 FIRST = (((0,), (0,)), ((), ()))
 LAST = (((1,), (1,)), ((), ()))
 
@@ -108,7 +108,9 @@
     groups = send_hbm.shape[0] // PIECE
     wide = packed_ref.shape[1]
     width = wide // 2
-    pairs = [(ids_hbm, ids_ref), (gates_hbm, gates_ref), (in_hbm, raw_ref)]
+    pairs = [(ids_hbm, ids_ref), (gates_hbm, gates_ref), (tokens_hbm, tokens_ref), (grad_hbm, grad_ref)]
+    small = len(pairs)
+    pairs.append((in_hbm, raw_ref))
     for i in range(model // wide):
         pairs.append(
             (
@@ -116,18 +118,9 @@
                 packed_ref.at[model + i * width : model + (i + 1) * width, :],
             )
         )
-    pairs += [(tokens_hbm, tokens_ref), (grad_hbm, grad_ref)]
     copies = start_all(pairs, sem)
-    copies[0].wait()
-    copies[1].wait()
+    wait_all(copies[:small])
     held, gate, _ = routing(ids_ref[...], gates_ref[...], groups)
-    wait_all(copies[2:-2])
-    raw = raw_ref[...]
-    packed_ref[:model, :width] = raw[:, 0, :]
-    packed_ref[:model, width:] = raw[:, 1, :]
-    leaving = pltpu.make_async_copy(packed_ref, packed_hbm, sem.at[0])
-    leaving.start()
-    wait_all(copies[-2:])
     rows = jnp.dot(held.astype(BF16), tokens_ref[...], preferred_element_type=F32).astype(BF16)
     grad = grad_ref[...]
     grad_rows = jnp.dot(
@@ -138,8 +131,12 @@
     weave_blocks(rows, grad_rows, wire_ref)
     sending = pltpu.make_async_copy(wire_ref, send_hbm, wire_sem)
     sending.start()
+    wait_all(copies[small:])
+    packed_ref[:model, :] = raw_ref[...].reshape(model, wide)
+    leaving = pltpu.make_async_copy(packed_ref, packed_hbm, sem.at[0])
+    leaving.start()
+    sending.wait()
     leaving.wait()
-    sending.wait()
 
 
 def assembly(sources, in_ref, out_ref):
@@ -205,53 +202,33 @@
         grad_pre_ref[:, r * wide + width : (r + 1) * wide] = (back_part * activated).astype(BF16)
     hidden = hidden_ref[...]
     grad_pre = grad_pre_ref[...]
+    order = (1, 2, 3, 0)
+    for r in order:
+        weight_grads(rows, grad_rows, hidden, grad_pre, r, grads[r])
+    leaving = start_all([(grads[r], grads_hbm[r]) for r in order], grad_sem)
     result = jnp.dot(hidden, out_ref[...], preferred_element_type=F32).astype(BF16)
     dx = lax.dot_general(grad_pre, in_ref[...], LAST, preferred_element_type=F32).astype(BF16)
     weave_blocks(result, dx, wire_ref)
     sending = pltpu.make_async_copy(wire_ref, back_hbm, sem)
     sending.start()
-    order = (1, 2, 3, 0)
-    for r in order:
-        weight_grads(rows, grad_rows, hidden, grad_pre, r, grads[r])
-    leaving = start_all([(grads[r], grads_hbm[r]) for r in order], grad_sem)
     sending.wait()
     wait_all(leaving)
 
 
-def finish_kernel(
-    wire_hbm, grad_hbm, ids_hbm, gates_hbm, partial_any, next_any, last_any,
-    mixed_ref, dx_ref, gate_grad_ref, in_hbm, out_hbm,
-    wire_ref, result_ref, back_ref, grad_ref, ids_ref, gates_ref,
-    partial_ref, next_ref, last_ref, in_ref, out_ref, sem, out_sem,
+def combine_kernel(
+    wire_hbm, grad_hbm, ids_hbm, gates_hbm, mixed_ref, dx_ref, gate_grad_ref,
+    wire_ref, result_ref, back_ref, grad_ref, ids_ref, gates_ref, sem,
 ):
     groups = result_ref.shape[0] // SLOTS
-    model = result_ref.shape[1]
-    wide = next_ref.shape[1]
-    width = wide // 2
     copies = start_all(
-        [(ids_hbm, ids_ref), (gates_hbm, gates_ref), (partial_any, partial_ref), (next_any, next_ref)]
-        + [(last_any, last_ref), (grad_hbm, grad_ref), (wire_hbm, wire_ref)],
-        sem,
+        [(ids_hbm, ids_ref), (gates_hbm, gates_ref), (grad_hbm, grad_ref), (wire_hbm, wire_ref)], sem
     )
     wait_all(copies[:2])
     ids = ids_ref[...]
     per_token, count_tok = ids.shape
     held, gate, expert = routing(ids, gates_ref[...], groups)
     mix = jnp.concatenate([part.astype(F32) for part in three_parts(gate)] + [held], axis=1).T.astype(BF16)
-
-    def total(lower, size):
-        value = partial_ref[lower : lower + size, :]
-        for piece in (next_ref, last_ref):
-            value = value + piece[lower : lower + size, :].astype(F32)
-        return value
-
     wait_all(copies[2:])
-    value = total(0, model)
-    in_ref[pl.ds(0, model, stride=2), :] = value[:, :width]
-    in_ref[pl.ds(1, model, stride=2), :] = value[:, width:]
-    for i in range(model // wide):
-        out_ref[:, i * wide : (i + 1) * wide] = total(model + i * width, width)
-    leaving = start_all([(in_ref, in_hbm), (out_ref, out_hbm)], out_sem)
     unweave_blocks(wire_ref, result_ref, back_ref)
     result = result_ref[...]
     gate_rows = 3 * count_tok
@@ -264,11 +241,29 @@
     for k in range(per_token):
         hit = ids[k : k + 1, :] == expert
         gate_grad_ref[k : k + 1, :] = jnp.sum(jnp.where(hit, inner, 0.0), axis=0, keepdims=True)
-    wait_all(leaving)
 
 
 def add_kernel(first_ref, second_ref, total_ref):
-    total_ref[...] = first_ref[...].astype(F32) + second_ref[...].astype(F32)
+    total_ref[...] = (first_ref[...].astype(F32) + second_ref[...].astype(F32)).astype(BF16)
+
+
+def reduce_kernel(*refs):
+    pieces, (in_ref, out_ref) = refs[:-2], refs[-2:]
+    wide = pieces[0].shape[1]
+    width = wide // 2
+    model = in_ref.shape[0] // 2
+
+    def total(lower, size):
+        value = pieces[0][lower : lower + size, :].astype(F32)
+        for piece in pieces[1:]:
+            value = value + piece[lower : lower + size, :].astype(F32)
+        return value
+
+    value = total(0, model)
+    in_ref[pl.ds(0, model, stride=2), :] = value[:, :width]
+    in_ref[pl.ds(1, model, stride=2), :] = value[:, width:]
+    for i in range(model // wide):
+        out_ref[:, i * wide : (i + 1) * wide] = total(model + i * width, width)
 
 
 def per_device(tokens, grad_out, expert_ids, gates, w_in, w_out):
@@ -280,11 +275,13 @@
     wide = 2 * width
     slots = groups * SLOTS
     wire = jax.ShapeDtypeStruct((groups * PIECE, model // 2), BF16)
-    params = pltpu.CompilerParams(vmem_limit_bytes=VMEM_LIMIT)
     in_hbm = pl.BlockSpec(memory_space=pltpu.HBM)
     anywhere = pl.BlockSpec(memory_space=pl.ANY)
     in_vmem = pl.BlockSpec(memory_space=pltpu.VMEM)
-    small = pltpu.CompilerParams(vmem_limit_bytes=4 * 1024 * 1024)
+
+    def room(mib):
+        return pltpu.CompilerParams(vmem_limit_bytes=mib * MIB)
+
 
     def shift(x, by):
         return lax.ppermute(x, "dp", [(i, (i + by) % replicas) for i in range(replicas)])
@@ -320,7 +317,7 @@
             pltpu.SemaphoreType.DMA((lines + 4,)),
             pltpu.SemaphoreType.DMA,
         ],
-        compiler_params=params,
+        compiler_params=room(10),
         name="dispatch",
     )(*[held_in(x, pltpu.HBM) for x in inputs])
     far = shift(packed, -2)
@@ -329,7 +326,7 @@
         out_shape=piece_like,
         in_specs=[anywhere],
         scratch_shapes=[pltpu.SemaphoreType.DMA((1,))],
-        compiler_params=small,
+        compiler_params=room(4),
         cost_estimate=pl.CostEstimate(flops=KEEP, bytes_accessed=0, transcendentals=0),
         name="keep",
     )(far)
@@ -349,42 +346,42 @@
             pltpu.SemaphoreType.DMA((replicas * lines,)),
             pltpu.SemaphoreType.DMA((replicas,)),
         ],
-        compiler_params=params,
+        compiler_params=room(20),
         name="expert",
     )(arrived, held_in(packed, pltpu.HBM), far_late, shift(packed, -1), shift(packed, 1))
     returned = exchange(back)
     partial = pl.pallas_call(
         add_kernel,
-        out_shape=jax.ShapeDtypeStruct(piece, F32),
-        compiler_params=params,
+        out_shape=jax.ShapeDtypeStruct(piece, BF16),
+        compiler_params=room(6),
         cost_estimate=pl.CostEstimate(flops=BESIDE, bytes_accessed=0, transcendentals=0),
         name="add",
     )(own, shift(grad_far, 2))
-    mixed, grad_tokens, gate_grad, sum_in, sum_out = pl.pallas_call(
-        finish_kernel,
+    mixed, grad_tokens, gate_grad = pl.pallas_call(
+        combine_kernel,
         out_shape=[
             jax.ShapeDtypeStruct(tokens.shape, BF16),
             jax.ShapeDtypeStruct(tokens.shape, BF16),
             jax.ShapeDtypeStruct((per_token, count_tok), F32),
-            pltpu.HBM((2 * model, width), F32),
-            pltpu.HBM((width, model), F32),
         ],
-        in_specs=[in_hbm] * 4 + [anywhere] * 3,
-        out_specs=[in_vmem] * 3 + [in_hbm] * 2,
+        in_specs=[in_hbm] * 4,
         scratch_shapes=[
             wire_like, rows_like, rows_like, tokens_like, ids_like, gates_like,
-            pltpu.VMEM(piece, F32), piece_like, piece_like,
-            pltpu.VMEM((2 * model, width), F32),
-            pltpu.VMEM((width, model), F32),
-            pltpu.SemaphoreType.DMA((7,)),
-            pltpu.SemaphoreType.DMA((2,)),
+            pltpu.SemaphoreType.DMA((4,)),
         ],
-        compiler_params=params,
-        name="finish",
-    )(
-        returned, *[held_in(x, pltpu.HBM) for x in (grad_out, ids_t, gates_t)],
-        partial, shift(grad_next, 1), shift(grad_last, -1),
-    )
+        compiler_params=room(8),
+        name="combine",
+    )(returned, *[held_in(x, pltpu.HBM) for x in (grad_out, ids_t, gates_t)])
+    partial, mixed = lax.optimization_barrier((partial, mixed))
+    sum_in, sum_out = pl.pallas_call(
+        reduce_kernel,
+        out_shape=[
+            jax.ShapeDtypeStruct((2 * model, width), F32),
+            jax.ShapeDtypeStruct((width, model), F32),
+        ],
+        compiler_params=room(8),
+        name="reduce",
+    )(partial, shift(grad_next, 1), shift(grad_last, -1))
     return mixed, grad_tokens, gate_grad.T, sum_in.reshape(1, model, 2, width), sum_out[None]
 
 

time: 113 us -> 111 us (0.982)
  local copies, waits for them, and re-layouts: 2.05 us -> 5.19 us
  waiting for transfers between devices: 46.1 us -> 43.3 us
  Pallas kernels: 15 us -> 13.2 us
    ppermute x6, waiting for transfers between devices: 35.6 us -> 18.8 us  [shift(): lax.ppermute(x, 'dp', [(i, (i + by) % replicas) for i in range(replicas)])]
    all_to_all x2, waiting for transfers between devices: 10.5 us -> 24.6 us  [exchange(): x = lax.all_to_all(x, 'expert', split_axis=0, concat_axis=0, tiled=True)]
    unnamed x6 -> x10, local copies, waits for them, and re-layouts: 2.05 us -> 5.19 us
    pallas_call x2 -> x3, Pallas kernels: 5.04 us -> 4.18 us  [the longest x1 2.69 us: per_device(): pl.pallas_call(combine_kernel, out_shape=[jax.ShapeDtypeStruct(tokens.sha...]
  transfers between devices with their start and end apart: 8 -> 8, of which waited for: 6 -> 5; matrix products, arithmetic and copies ran while one was open for 0% -> 0% of each run, Pallas kernels for 0% -> 3%
where the time goes in v3:
time: 111 us; the launch traced here: 110 us
  starting transfers between devices  47.4 us (43%)
  waiting for transfers between devices  43.3 us (39%)
  Pallas kernels  13.2 us (12%)
  local copies, waits for them, and re-layouts  5.19 us (5%)
    all_to_all x2, starting transfers between devices, exchange(): x = lax.all_to_all(x, 'expert', split_axis=0, concat_axis=0, tiled=True)  26.8 us
    all_to_all x2, waiting for transfers between devices, exchange(): x = lax.all_to_all(x, 'expert', split_axis=0, concat_axis=0, tiled=True)  24.6 us
    ppermute x6, starting transfers between devices, shift(): lax.ppermute(x, 'dp', [(i, (i + by) % replicas) for i in range(replicas)])  20.6 us
    ppermute x6, waiting for transfers between devices, shift(): lax.ppermute(x, 'dp', [(i, (i + by) % replicas) for i in range(replicas)])  18.8 us
    pallas_call x1, Pallas kernels, per_device(): pl.pallas_call(lambda *refs: expert_kernel(replicas, *refs), out_shape=[p...  5.6 us
    unnamed x10, local copies, waits for them, and re-layouts  5.19 us
    pallas_call x1, Pallas kernels, per_device(): pl.pallas_call(dispatch_kernel, out_shape=[pltpu.HBM(piece, BF16), pltpu....  3.32 us
    pallas_call x1, Pallas kernels, per_device(): pl.pallas_call(combine_kernel, out_shape=[jax.ShapeDtypeStruct(tokens.sha...  2.69 us
  transfers between devices with their start and end apart: 8, of which 5 were waited for; matrix products, arithmetic and copies ran while one was open for 0% of the time, Pallas kernels for 3%

profile of v3, /device:TPU:1, one launch (start us, length us, event | category | flops | bytes accessed | tf_op | source)
XLA Modules:
  0.0 109.8 jit_solution(5125040132104040700)
XLA Ops:
  0.6 3.3 %dispatch.1 = (bf16[1536,256]{1,0:T(8,128)(2,1)}, bf16[1024,512]{1,0:T(8,128)(2,1)}) custom-call(bf16[1024,2,128]{2,1,0:T(2,128)(2,1)} %bitcast.15, bf16[128,1024]{1,0:T(8,128)(2,1)} %bitcast.16, bf16[24,1024]{1,0:T(8,128)(2,1)} %tokens_hbm.1, bf16[24,1024]{1,0:T(8,128)(2,1)} %grad_hbm.3, s32[8,24]{1,0:T(8,128)} %bitcast.17, f32[8,24]{1,0:T(8,128)} %bitcast.19), custom_call_target="tpu_custom_call" | custom-call | tf_op jit(solution)/shard_map/dispatch/pallas_call | solution.py:309
  4.0 5.5 %collective-permute-start = (bf16[1536,256]{1,0:T(8,128)(2,1)}, bf16[1536,256]{1,0:T(8,128)(2,1)S(1)}, u32[]{:S(2)}, u32[]{:S(2)}) collective-permute-start(bf16[1536,256]{1,0:T(8,128)(2,1)} %get-tuple-element.20.refs_1_), channel_id=1, source_target_pairs={{0,256},{128,384},{256,0},{384,128},{1,257},{129,385},{257,1},{385... | collective-permute-start | bytes 2359304 | tf_op jit(solution)/shard_map/ppermute | solution.py:287
  9.4 17.9 %all-to-all-start = ((bf16[128,8,512]{2,1,0:T(8,128)(2,1)}), bf16[128,8,512]{2,1,0:T(8,128)(2,1)S(1)}, u32[]{:S(2)}, u32[]{:S(2)}) async-start(bf16[128,8,512]{2,1,0:T(8,128)(2,1)} %bitcast.14), calls=%async_computation | async-start | bytes 2097152 | tf_op jit(solution)/shard_map/all_to_all | solution.py:294
  27.3 2.2 %collective-permute-start.2 = (bf16[1536,256]{1,0:T(8,128)(2,1)}, bf16[1536,256]{1,0:T(8,128)(2,1)S(1)}, u32[]{:S(2)}, u32[]{:S(2)}) collective-permute-start(bf16[1536,256]{1,0:T(8,128)(2,1)} %get-tuple-element.20.refs_1_), channel_id=1, source_target_pairs={{0,128},{128,256},{256,384},{384,0},{1,129},{129,257},{257,385},{3... | collective-permute-start | bytes 2359304 | tf_op jit(solution)/shard_map/ppermute | solution.py:287
  29.6 4.3 %collective-permute-start.1 = (bf16[1536,256]{1,0:T(8,128)(2,1)}, bf16[1536,256]{1,0:T(8,128)(2,1)S(1)}, u32[]{:S(2)}, u32[]{:S(2)}) collective-permute-start(bf16[1536,256]{1,0:T(8,128)(2,1)} %get-tuple-element.20.refs_1_), channel_id=1, source_target_pairs={{0,384},{128,0},{256,128},{384,256},{1,385},{129,1},{257,129},{385... | collective-permute-start | bytes 2359304 | tf_op jit(solution)/shard_map/ppermute | solution.py:287
  33.8 0.0 collective-permute-done.far_hbm
  33.9 0.0 copy-start.3
  33.9 0.9 copy-done.3
  34.8 0.0 copy-start.4
  34.8 1.1 %copy-done.4 = bf16[1536,256]{1,0:T(8,128)(2,1)S(1)} copy-done((bf16[1536,256]{1,0:T(8,128)(2,1)S(1)}, bf16[1536,256]{1,0:T(8,128)(2,1)}, u32[]{:S(2)}) %copy-start.4) | copy-done | bytes 786456
  35.9 0.1 keep.1.refs_2_
  36.0 12.8 %collective-permute-done.2.refs_4_ = bf16[1536,256]{1,0:T(8,128)(2,1)S(1)} collective-permute-done((bf16[1536,256]{1,0:T(8,128)(2,1)}, bf16[1536,256]{1,0:T(8,128)(2,1)S(1)}, u32[]{:S(2)}, u32[]{:S(2)}) %collective-permute-start.2) | collective-permute-done | bytes 786464 | tf_op jit(solution)/shard_map/ppermute | solution.py:287
  48.8 1.0 collective-permute-done.1.refs_3_
  49.8 8.4 %all-to-all-done = bf16[128,8,512]{2,1,0:T(8,128)(2,1)S(1)} async-done(((bf16[128,8,512]{2,1,0:T(8,128)(2,1)}), bf16[128,8,512]{2,1,0:T(8,128)(2,1)S(1)}, u32[]{:S(2)}, u32[]{:S(2)}) %all-to-all-start) | async-done | bytes 1048608 | tf_op jit(solution)/shard_map/all_to_all | solution.py:294
  58.2 5.6 %expert.1 = (bf16[1024,512]{1,0:T(8,128)(2,1)}, bf16[1536,256]{1,0:T(8,128)(2,1)}, bf16[1536,256]{1,0:T(8,128)(2,1)}, bf16[1536,256]{1,0:T(8,128)(2,1)}, bf16[1536,256]{1,0:T(8,128)(2,1)}) custom-call(bf16[1024,512]{1,0:T(8,128)(2,1)S(1)} %bitcast.12, bf16[1536,256]{1,0:T(8,128)(2,1)} %get-tuple-element.20.refs_1_, bf16[1536,256]{1,0:T(8,128)(2,1)S(1)} %keep.1.refs_2_, ...), custom_call_target="tpu_custom_call" | custom-call | tf_op jit(solution)/shard_map/expert/pallas_call | solution.py:335
  63.8 2.1 %collective-permute-start.3 = (bf16[1536,256]{1,0:T(8,128)(2,1)}, bf16[1536,256]{1,0:T(8,128)(2,1)S(1)}, u32[]{:S(2)}, u32[]{:S(2)}) collective-permute-start(bf16[1536,256]{1,0:T(8,128)(2,1)} %get-tuple-element.22), channel_id=1, source_target_pairs={{0,256},{128,384},{256,0},{384,128},{1,257},{129,385},{257,1},{385... | collective-permute-start | bytes 2359304 | tf_op jit(solution)/shard_map/ppermute | solution.py:287
  66.0 8.9 %all-to-all-start.1 = ((bf16[128,8,512]{2,1,0:T(8,128)(2,1)}), bf16[128,8,512]{2,1,0:T(8,128)(2,1)S(1)}, u32[]{:S(2)}, u32[]{:S(2)}) async-start(bf16[128,8,512]{2,1,0:T(8,128)(2,1)} %bitcast.13), calls=%async_computation.1 | async-start | bytes 2097152 | tf_op jit(solution)/shard_map/all_to_all | solution.py:294
  74.9 4.0 %collective-permute-start.4 = (bf16[1536,256]{1,0:T(8,128)(2,1)}, bf16[1536,256]{1,0:T(8,128)(2,1)S(1)}, u32[]{:S(2)}, u32[]{:S(2)}) collective-permute-start(bf16[1536,256]{1,0:T(8,128)(2,1)} %get-tuple-element.29), channel_id=1, source_target_pairs={{0,128},{128,256},{256,384},{384,0},{1,129},{129,257},{257,385},{3... | collective-permute-start | bytes 2359304 | tf_op jit(solution)/shard_map/ppermute | solution.py:287
  78.9 2.5 %collective-permute-start.5 = (bf16[1536,256]{1,0:T(8,128)(2,1)}, bf16[1536,256]{1,0:T(8,128)(2,1)S(1)}, u32[]{:S(2)}, u32[]{:S(2)}) collective-permute-start(bf16[1536,256]{1,0:T(8,128)(2,1)} %get-tuple-element.30), channel_id=1, source_target_pairs={{0,384},{128,0},{256,128},{384,256},{1,385},{129,1},{257,129},{385... | collective-permute-start | bytes 2359304 | tf_op jit(solution)/shard_map/ppermute | solution.py:287
  81.4 4.9 %collective-permute-done.3.second_ref = bf16[1536,256]{1,0:T(8,128)(2,1)S(1)} collective-permute-done((bf16[1536,256]{1,0:T(8,128)(2,1)}, bf16[1536,256]{1,0:T(8,128)(2,1)S(1)}, u32[]{:S(2)}, u32[]{:S(2)}) %collective-permute-start.3) | collective-permute-done | bytes 786464 | tf_op jit(solution)/shard_map/ppermute | solution.py:287
  86.4 0.0 copy-start.1
  86.4 0.9 copy-done.1
  87.3 0.0 copy-start
  87.3 1.1 %copy-done = bf16[1536,256]{1,0:T(8,128)(2,1)S(1)} copy-done((bf16[1536,256]{1,0:T(8,128)(2,1)S(1)}, bf16[1536,256]{1,0:T(8,128)(2,1)}, u32[]{:S(2)}) %copy-start) | copy-done | bytes 786456
  88.4 0.0 copy-start.2
  88.4 1.1 %copy-done.2 = bf16[1536,256]{1,0:T(8,128)(2,1)S(1)} copy-done((bf16[1536,256]{1,0:T(8,128)(2,1)S(1)}, bf16[1536,256]{1,0:T(8,128)(2,1)}, u32[]{:S(2)}) %copy-start.2) | copy-done | bytes 786456
  89.5 0.2 add.1.refs_0_
  89.7 16.1 %all-to-all-done.1 = bf16[128,8,512]{2,1,0:T(8,128)(2,1)S(1)} async-done(((bf16[128,8,512]{2,1,0:T(8,128)(2,1)}), bf16[128,8,512]{2,1,0:T(8,128)(2,1)S(1)}, u32[]{:S(2)}, u32[]{:S(2)}) %all-to-all-start.1) | async-done | bytes 1048608 | tf_op jit(solution)/shard_map/all_to_all | solution.py:294
  105.8 2.7 %combine.1 = (bf16[24,1024]{1,0:T(8,128)(2,1)}, bf16[24,1024]{1,0:T(8,128)(2,1)}, f32[8,24]{1,0:T(8,128)}) custom-call(bf16[1024,512]{1,0:T(8,128)(2,1)S(1)} %bitcast.11, bf16[24,1024]{1,0:T(8,128)(2,1)} %grad_hbm.3, s32[8,24]{1,0:T(8,128)} %bitcast.18, f32[8,24]{1,0:T(8,128)} %bitcast.20), custom_call_target="tpu_custom_call" | custom-call | tf_op jit(solution)/shard_map/combine/pallas_call | solution.py:360
  108.5 0.0 collective-permute-done.4.refs_1_
  108.5 0.0 collective-permute-done.5.refs_2_
  108.5 1.3 %reduce.1 = (f32[2048,128]{1,0:T(8,128)}, f32[128,1024]{1,0:T(8,128)}) custom-call(bf16[1536,256]{1,0:T(8,128)(2,1)S(1)} %add.1.refs_0_, bf16[1536,256]{1,0:T(8,128)(2,1)S(1)} %collective-permute-done.4.refs_1_, bf16[1536,256]{1,0:T(8,128)(2,1)S(1)} %collective-permute-done.5.refs_2_), custom_call_target="tpu_custom_call" | custom-call | tf_op jit(solution)/shard_map/reduce/pallas_call | solution.py:376
Async XLA Ops:
  4.0 29.9 %collective-permute-start = (bf16[1536,256]{1,0:T(8,128)(2,1)}, bf16[1536,256]{1,0:T(8,128)(2,1)S(1)}, u32[]{:S(2)}, u32[]{:S(2)}) collective-permute-start(bf16[1536,256]{1,0:T(8,128)(2,1)} %get-tuple-element.20.refs_1_), channel_id=1, source_target_pairs={{0,256},{128,384},{256,0},{384,128},{1,257},{129,385},{257,1},{385... | collective-permute-start | bytes 2359304 | tf_op jit(solution)/shard_map/ppermute | solution.py:287
  9.4 48.8 %all-to-all-start = ((bf16[128,8,512]{2,1,0:T(8,128)(2,1)}), bf16[128,8,512]{2,1,0:T(8,128)(2,1)S(1)}, u32[]{:S(2)}, u32[]{:S(2)}) async-start(bf16[128,8,512]{2,1,0:T(8,128)(2,1)} %bitcast.14), calls=%async_computation | async-start | bytes 2097152 | tf_op jit(solution)/shard_map/all_to_all | solution.py:294
  27.3 21.5 %collective-permute-start.2 = (bf16[1536,256]{1,0:T(8,128)(2,1)}, bf16[1536,256]{1,0:T(8,128)(2,1)S(1)}, u32[]{:S(2)}, u32[]{:S(2)}) collective-permute-start(bf16[1536,256]{1,0:T(8,128)(2,1)} %get-tuple-element.20.refs_1_), channel_id=1, source_target_pairs={{0,128},{128,256},{256,384},{384,0},{1,129},{129,257},{257,385},{3... | collective-permute-start | bytes 2359304 | tf_op jit(solution)/shard_map/ppermute | solution.py:287
  29.6 20.2 %collective-permute-start.1 = (bf16[1536,256]{1,0:T(8,128)(2,1)}, bf16[1536,256]{1,0:T(8,128)(2,1)S(1)}, u32[]{:S(2)}, u32[]{:S(2)}) collective-permute-start(bf16[1536,256]{1,0:T(8,128)(2,1)} %get-tuple-element.20.refs_1_), channel_id=1, source_target_pairs={{0,384},{128,0},{256,128},{384,256},{1,385},{129,1},{257,129},{385... | collective-permute-start | bytes 2359304 | tf_op jit(solution)/shard_map/ppermute | solution.py:287
  33.9 0.9 copy-start.3
  34.8 1.1 %copy-start.4 = (bf16[1536,256]{1,0:T(8,128)(2,1)S(1)}, bf16[1536,256]{1,0:T(8,128)(2,1)}, u32[]{:S(2)}) copy-start(bf16[1536,256]{1,0:T(8,128)(2,1)} %copy-done.3) | copy-start | bytes 2359300
  63.8 22.5 %collective-permute-start.3 = (bf16[1536,256]{1,0:T(8,128)(2,1)}, bf16[1536,256]{1,0:T(8,128)(2,1)S(1)}, u32[]{:S(2)}, u32[]{:S(2)}) collective-permute-start(bf16[1536,256]{1,0:T(8,128)(2,1)} %get-tuple-element.22), channel_id=1, source_target_pairs={{0,256},{128,384},{256,0},{384,128},{1,257},{129,385},{257,1},{385... | collective-permute-start | bytes 2359304 | tf_op jit(solution)/shard_map/ppermute | solution.py:287
  66.0 39.8 %all-to-all-start.1 = ((bf16[128,8,512]{2,1,0:T(8,128)(2,1)}), bf16[128,8,512]{2,1,0:T(8,128)(2,1)S(1)}, u32[]{:S(2)}, u32[]{:S(2)}) async-start(bf16[128,8,512]{2,1,0:T(8,128)(2,1)} %bitcast.13), calls=%async_computation.1 | async-start | bytes 2097152 | tf_op jit(solution)/shard_map/all_to_all | solution.py:294
  74.9 33.6 %collective-permute-start.4 = (bf16[1536,256]{1,0:T(8,128)(2,1)}, bf16[1536,256]{1,0:T(8,128)(2,1)S(1)}, u32[]{:S(2)}, u32[]{:S(2)}) collective-permute-start(bf16[1536,256]{1,0:T(8,128)(2,1)} %get-tuple-element.29), channel_id=1, source_target_pairs={{0,128},{128,256},{256,384},{384,0},{1,129},{129,257},{257,385},{3... | collective-permute-start | bytes 2359304 | tf_op jit(solution)/shard_map/ppermute | solution.py:287
  78.9 29.6 %collective-permute-start.5 = (bf16[1536,256]{1,0:T(8,128)(2,1)}, bf16[1536,256]{1,0:T(8,128)(2,1)S(1)}, u32[]{:S(2)}, u32[]{:S(2)}) collective-permute-start(bf16[1536,256]{1,0:T(8,128)(2,1)} %get-tuple-element.30), channel_id=1, source_target_pairs={{0,384},{128,0},{256,128},{384,256},{1,385},{129,1},{257,129},{385... | collective-permute-start | bytes 2359304 | tf_op jit(solution)/shard_map/ppermute | solution.py:287
  86.4 0.9 copy-start.1
  87.3 1.1 %copy-start = (bf16[1536,256]{1,0:T(8,128)(2,1)S(1)}, bf16[1536,256]{1,0:T(8,128)(2,1)}, u32[]{:S(2)}) copy-start(bf16[1536,256]{1,0:T(8,128)(2,1)} %get-tuple-element.21.first_ref) | copy-start | bytes 2359300
  88.4 1.1 %copy-start.2 = (bf16[1536,256]{1,0:T(8,128)(2,1)S(1)}, bf16[1536,256]{1,0:T(8,128)(2,1)}, u32[]{:S(2)}) copy-start(bf16[1536,256]{1,0:T(8,128)(2,1)} %copy-done.1) | copy-start | bytes 2359300

commit v4 on v3

--- a/solution.py
+++ b/solution.py
@@ -243,7 +243,8 @@
         gate_grad_ref[k : k + 1, :] = jnp.sum(jnp.where(hit, inner, 0.0), axis=0, keepdims=True)
 
 
-def add_kernel(first_ref, second_ref, total_ref):
+def add_kernel(first_hbm, second_hbm, total_ref, first_ref, second_ref, sem):
+    wait_all(start_all([(first_hbm, first_ref), (second_hbm, second_ref)], sem))
     total_ref[...] = (first_ref[...].astype(F32) + second_ref[...].astype(F32)).astype(BF16)
 
 
@@ -329,7 +330,7 @@
         compiler_params=room(4),
         cost_estimate=pl.CostEstimate(flops=KEEP, bytes_accessed=0, transcendentals=0),
         name="keep",
-    )(far)
+    )(held_in(far, pltpu.HBM))
     arrived = exchange(send)
 
     back, own, grad_far, grad_next, grad_last = pl.pallas_call(
@@ -353,10 +354,12 @@
     partial = pl.pallas_call(
         add_kernel,
         out_shape=jax.ShapeDtypeStruct(piece, BF16),
+        in_specs=[in_hbm] * 2,
+        scratch_shapes=[piece_like, piece_like, pltpu.SemaphoreType.DMA((2,))],
         compiler_params=room(6),
         cost_estimate=pl.CostEstimate(flops=BESIDE, bytes_accessed=0, transcendentals=0),
         name="add",
-    )(own, shift(grad_far, 2))
+    )(held_in(own, pltpu.HBM), held_in(shift(grad_far, 2), pltpu.HBM))
     mixed, grad_tokens, gate_grad = pl.pallas_call(
         combine_kernel,
         out_shape=[
@@ -364,14 +367,14 @@
             jax.ShapeDtypeStruct(tokens.shape, BF16),
             jax.ShapeDtypeStruct((per_token, count_tok), F32),
         ],
-        in_specs=[in_hbm] * 4,
+        in_specs=[anywhere] * 4,
         scratch_shapes=[
             wire_like, rows_like, rows_like, tokens_like, ids_like, gates_like,
             pltpu.SemaphoreType.DMA((4,)),
         ],
         compiler_params=room(8),
         name="combine",
-    )(returned, *[held_in(x, pltpu.HBM) for x in (grad_out, ids_t, gates_t)])
+    )(returned, grad_out, ids_t, gates_t)
     partial, mixed = lax.optimization_barrier((partial, mixed))
     sum_in, sum_out = pl.pallas_call(
         reduce_kernel,

time: 111 us -> 110 us (level)
  local copies, waits for them, and re-layouts: 5.19 us -> 0.91 us
  waiting for transfers between devices: 43.3 us -> 45.2 us
  Pallas kernels: 13.2 us -> 15.1 us
    unnamed x10 -> x8, local copies, waits for them, and re-layouts: 5.19 us -> 0.91 us
    pallas_call x1, Pallas kernels: 0.18 us -> 1.57 us  [per_device(): pl.pallas_call(add_kernel, out_shape=jax.ShapeDtypeStruct(piece, BF16), i...]
  transfers between devices with their start and end apart: 8 -> 8, of which waited for: 5 -> 5; matrix products, arithmetic and copies ran while one was open for 0% -> 0% of each run, Pallas kernels for 3% -> 4%
where the time goes in v4:
time: 110 us; the launch traced here: 109 us
  starting transfers between devices  47.4 us (43%)
  waiting for transfers between devices  45.2 us (41%)
  Pallas kernels  15.1 us (14%)
    all_to_all x2, starting transfers between devices, exchange(): x = lax.all_to_all(x, 'expert', split_axis=0, concat_axis=0, tiled=True)  26.8 us
    all_to_all x2, waiting for transfers between devices, exchange(): x = lax.all_to_all(x, 'expert', split_axis=0, concat_axis=0, tiled=True)  25.4 us
    ppermute x6, starting transfers between devices, shift(): lax.ppermute(x, 'dp', [(i, (i + by) % replicas) for i in range(replicas)])  20.6 us
    ppermute x6, waiting for transfers between devices, shift(): lax.ppermute(x, 'dp', [(i, (i + by) % replicas) for i in range(replicas)])  19.7 us
    pallas_call x1, Pallas kernels, per_device(): pl.pallas_call(lambda *refs: expert_kernel(replicas, *refs), out_shape=[p...  5.6 us
    pallas_call x1, Pallas kernels, per_device(): pl.pallas_call(dispatch_kernel, out_shape=[pltpu.HBM(piece, BF16), pltpu....  3.32 us
  transfers between devices with their start and end apart: 8, of which 5 were waited for; matrix products, arithmetic and copies ran while one was open for 0% of the time, Pallas kernels for 4%

profile of v4, /device:TPU:1, one launch (start us, length us, event | category | flops | bytes accessed | tf_op | source)
XLA Modules:
  0.0 109.3 jit_solution(3198635755014677079)
XLA Ops:
  0.6 3.3 %dispatch.1 = (bf16[1536,256]{1,0:T(8,128)(2,1)}, bf16[1024,512]{1,0:T(8,128)(2,1)}) custom-call(bf16[1024,2,128]{2,1,0:T(2,128)(2,1)} %bitcast.19, bf16[128,1024]{1,0:T(8,128)(2,1)} %bitcast.20, bf16[24,1024]{1,0:T(8,128)(2,1)} %tokens_hbm.1, bf16[24,1024]{1,0:T(8,128)(2,1)} %grad_hbm.3, s32[8,24]{1,0:T(8,128)} %bitcast.13, f32[8,24]{1,0:T(8,128)} %bitcast.15), custom_call_target="tpu_custom_call" | custom-call | tf_op jit(solution)/shard_map/dispatch/pallas_call | solution.py:310
  4.0 5.5 %collective-permute-start = (bf16[1536,256]{1,0:T(8,128)(2,1)}, bf16[1536,256]{1,0:T(8,128)(2,1)}, u32[]{:S(2)}, u32[]{:S(2)}) collective-permute-start(bf16[1536,256]{1,0:T(8,128)(2,1)} %get-tuple-element.20.refs_1_), channel_id=1, source_target_pairs={{0,256},{128,384},{256,0},{384,128},{1,257},{129,385},{257,1},{385... | collective-permute-start | bytes 2359304 | tf_op jit(solution)/shard_map/ppermute | solution.py:288
  9.5 17.9 %all-to-all-start = ((bf16[128,8,512]{2,1,0:T(8,128)(2,1)}), bf16[128,8,512]{2,1,0:T(8,128)(2,1)S(1)}, u32[]{:S(2)}, u32[]{:S(2)}) async-start(bf16[128,8,512]{2,1,0:T(8,128)(2,1)} %bitcast.18), calls=%async_computation | async-start | bytes 2097152 | tf_op jit(solution)/shard_map/all_to_all | solution.py:295
  27.3 2.2 %collective-permute-start.2 = (bf16[1536,256]{1,0:T(8,128)(2,1)}, bf16[1536,256]{1,0:T(8,128)(2,1)S(1)}, u32[]{:S(2)}, u32[]{:S(2)}) collective-permute-start(bf16[1536,256]{1,0:T(8,128)(2,1)} %get-tuple-element.20.refs_1_), channel_id=1, source_target_pairs={{0,128},{128,256},{256,384},{384,0},{1,129},{129,257},{257,385},{3... | collective-permute-start | bytes 2359304 | tf_op jit(solution)/shard_map/ppermute | solution.py:288
  29.6 4.3 %collective-permute-start.1 = (bf16[1536,256]{1,0:T(8,128)(2,1)}, bf16[1536,256]{1,0:T(8,128)(2,1)S(1)}, u32[]{:S(2)}, u32[]{:S(2)}) collective-permute-start(bf16[1536,256]{1,0:T(8,128)(2,1)} %get-tuple-element.20.refs_1_), channel_id=1, source_target_pairs={{0,384},{128,0},{256,128},{384,256},{1,385},{129,1},{257,129},{385... | collective-permute-start | bytes 2359304 | tf_op jit(solution)/shard_map/ppermute | solution.py:288
  33.9 0.0 collective-permute-done.far_hbm
  33.9 1.1 %keep.1.refs_2_ = bf16[1536,256]{1,0:T(8,128)(2,1)S(1)} custom-call(bf16[1536,256]{1,0:T(8,128)(2,1)} %collective-permute-done.far_hbm), custom_call_target="tpu_custom_call" | custom-call | flops 19000000512 | tf_op jit(solution)/shard_map/keep/pallas_call | solution.py:325
  35.0 13.8 %collective-permute-done.2.refs_4_ = bf16[1536,256]{1,0:T(8,128)(2,1)S(1)} collective-permute-done((bf16[1536,256]{1,0:T(8,128)(2,1)}, bf16[1536,256]{1,0:T(8,128)(2,1)S(1)}, u32[]{:S(2)}, u32[]{:S(2)}) %collective-permute-start.2) | collective-permute-done | bytes 786464 | tf_op jit(solution)/shard_map/ppermute | solution.py:288
  48.8 1.0 collective-permute-done.1.refs_3_
  49.8 8.4 %all-to-all-done = bf16[128,8,512]{2,1,0:T(8,128)(2,1)S(1)} async-done(((bf16[128,8,512]{2,1,0:T(8,128)(2,1)}), bf16[128,8,512]{2,1,0:T(8,128)(2,1)S(1)}, u32[]{:S(2)}, u32[]{:S(2)}) %all-to-all-start) | async-done | bytes 1048608 | tf_op jit(solution)/shard_map/all_to_all | solution.py:295
  58.2 5.6 %expert.1 = (bf16[1024,512]{1,0:T(8,128)(2,1)}, bf16[1536,256]{1,0:T(8,128)(2,1)}, bf16[1536,256]{1,0:T(8,128)(2,1)}, bf16[1536,256]{1,0:T(8,128)(2,1)}, bf16[1536,256]{1,0:T(8,128)(2,1)}) custom-call(bf16[1024,512]{1,0:T(8,128)(2,1)S(1)} %bitcast.12, bf16[1536,256]{1,0:T(8,128)(2,1)} %get-tuple-element.20.refs_1_, bf16[1536,256]{1,0:T(8,128)(2,1)S(1)} %keep.1.refs_2_, ...), custom_call_target="tpu_custom_call" | custom-call | tf_op jit(solution)/shard_map/expert/pallas_call | solution.py:336
  63.9 2.1 %collective-permute-start.3 = (bf16[1536,256]{1,0:T(8,128)(2,1)}, bf16[1536,256]{1,0:T(8,128)(2,1)S(1)}, u32[]{:S(2)}, u32[]{:S(2)}) collective-permute-start(bf16[1536,256]{1,0:T(8,128)(2,1)} %get-tuple-element.22), channel_id=1, source_target_pairs={{0,256},{128,384},{256,0},{384,128},{1,257},{129,385},{257,1},{385... | collective-permute-start | bytes 2359304 | tf_op jit(solution)/shard_map/ppermute | solution.py:288
  66.0 8.9 %all-to-all-start.1 = ((bf16[128,8,512]{2,1,0:T(8,128)(2,1)}), bf16[128,8,512]{2,1,0:T(8,128)(2,1)S(1)}, u32[]{:S(2)}, u32[]{:S(2)}) async-start(bf16[128,8,512]{2,1,0:T(8,128)(2,1)} %bitcast.17), calls=%async_computation.1 | async-start | bytes 2097152 | tf_op jit(solution)/shard_map/all_to_all | solution.py:295
  74.9 4.0 %collective-permute-start.4 = (bf16[1536,256]{1,0:T(8,128)(2,1)}, bf16[1536,256]{1,0:T(8,128)(2,1)S(1)}, u32[]{:S(2)}, u32[]{:S(2)}) collective-permute-start(bf16[1536,256]{1,0:T(8,128)(2,1)} %get-tuple-element.29), channel_id=1, source_target_pairs={{0,128},{128,256},{256,384},{384,0},{1,129},{129,257},{257,385},{3... | collective-permute-start | bytes 2359304 | tf_op jit(solution)/shard_map/ppermute | solution.py:288
  78.9 2.5 %collective-permute-start.5 = (bf16[1536,256]{1,0:T(8,128)(2,1)}, bf16[1536,256]{1,0:T(8,128)(2,1)S(1)}, u32[]{:S(2)}, u32[]{:S(2)}) collective-permute-start(bf16[1536,256]{1,0:T(8,128)(2,1)} %get-tuple-element.30), channel_id=1, source_target_pairs={{0,384},{128,0},{256,128},{384,256},{1,385},{129,1},{257,129},{385... | collective-permute-start | bytes 2359304 | tf_op jit(solution)/shard_map/ppermute | solution.py:288
  81.4 4.9 %collective-permute-done.3.second_hbm = bf16[1536,256]{1,0:T(8,128)(2,1)S(1)} collective-permute-done((bf16[1536,256]{1,0:T(8,128)(2,1)}, bf16[1536,256]{1,0:T(8,128)(2,1)S(1)}, u32[]{:S(2)}, u32[]{:S(2)}) %collective-permute-start.3) | collective-permute-done | bytes 786464 | tf_op jit(solution)/shard_map/ppermute | solution.py:288
  86.4 0.0 copy-start.3
  86.4 0.9 copy-done.3
  87.3 0.0 copy-start
  87.3 0.0 copy-start.1
  87.3 0.0 copy-start.2
  87.3 1.6 %add.1.refs_0_ = bf16[1536,256]{1,0:T(8,128)(2,1)S(1)} custom-call(bf16[1536,256]{1,0:T(8,128)(2,1)} %get-tuple-element.21.first_hbm, bf16[1536,256]{1,0:T(8,128)(2,1)} %copy-done.3), custom_call_target="tpu_custom_call" | custom-call | flops 99999997952 | tf_op jit(solution)/shard_map/add/pallas_call | solution.py:354
  88.9 17.0 %all-to-all-done.1 = bf16[128,8,512]{2,1,0:T(8,128)(2,1)S(1)} async-done(((bf16[128,8,512]{2,1,0:T(8,128)(2,1)}), bf16[128,8,512]{2,1,0:T(8,128)(2,1)S(1)}, u32[]{:S(2)}, u32[]{:S(2)}) %all-to-all-start.1) | async-done | bytes 1048608 | tf_op jit(solution)/shard_map/all_to_all | solution.py:295
  105.8 0.0 copy-done
  105.8 0.0 copy-done.1
  105.8 0.0 copy-done.2
  105.8 2.2 %combine.1 = (bf16[24,1024]{1,0:T(8,128)(2,1)}, bf16[24,1024]{1,0:T(8,128)(2,1)}, f32[8,24]{1,0:T(8,128)}) custom-call(bf16[1024,512]{1,0:T(8,128)(2,1)S(1)} %bitcast.11, bf16[24,1024]{1,0:T(8,128)(2,1)S(1)} %copy-done, s32[8,24]{1,0:T(8,128)S(1)} %bitcast.14, f32[8,24]{1,0:T(8,128)S(1)} %bitcast.16), custom_call_target="tpu_custom_call" | custom-call | tf_op jit(solution)/shard_map/combine/pallas_call | solution.py:363
  108.0 0.0 collective-permute-done.4.refs_1_
  108.0 0.0 collective-permute-done.5.refs_2_
  108.0 1.3 %reduce.1 = (f32[2048,128]{1,0:T(8,128)}, f32[128,1024]{1,0:T(8,128)}) custom-call(bf16[1536,256]{1,0:T(8,128)(2,1)S(1)} %add.1.refs_0_, bf16[1536,256]{1,0:T(8,128)(2,1)S(1)} %collective-permute-done.4.refs_1_, bf16[1536,256]{1,0:T(8,128)(2,1)S(1)} %collective-permute-done.5.refs_2_), custom_call_target="tpu_custom_call" | custom-call | tf_op jit(solution)/shard_map/reduce/pallas_call | solution.py:379
Async XLA Ops:
  4.0 29.9 %collective-permute-start = (bf16[1536,256]{1,0:T(8,128)(2,1)}, bf16[1536,256]{1,0:T(8,128)(2,1)}, u32[]{:S(2)}, u32[]{:S(2)}) collective-permute-start(bf16[1536,256]{1,0:T(8,128)(2,1)} %get-tuple-element.20.refs_1_), channel_id=1, source_target_pairs={{0,256},{128,384},{256,0},{384,128},{1,257},{129,385},{257,1},{385... | collective-permute-start | bytes 2359304 | tf_op jit(solution)/shard_map/ppermute | solution.py:288
  9.5 48.8 %all-to-all-start = ((bf16[128,8,512]{2,1,0:T(8,128)(2,1)}), bf16[128,8,512]{2,1,0:T(8,128)(2,1)S(1)}, u32[]{:S(2)}, u32[]{:S(2)}) async-start(bf16[128,8,512]{2,1,0:T(8,128)(2,1)} %bitcast.18), calls=%async_computation | async-start | bytes 2097152 | tf_op jit(solution)/shard_map/all_to_all | solution.py:295
  27.3 21.5 %collective-permute-start.2 = (bf16[1536,256]{1,0:T(8,128)(2,1)}, bf16[1536,256]{1,0:T(8,128)(2,1)S(1)}, u32[]{:S(2)}, u32[]{:S(2)}) collective-permute-start(bf16[1536,256]{1,0:T(8,128)(2,1)} %get-tuple-element.20.refs_1_), channel_id=1, source_target_pairs={{0,128},{128,256},{256,384},{384,0},{1,129},{129,257},{257,385},{3... | collective-permute-start | bytes 2359304 | tf_op jit(solution)/shard_map/ppermute | solution.py:288
  29.6 20.2 %collective-permute-start.1 = (bf16[1536,256]{1,0:T(8,128)(2,1)}, bf16[1536,256]{1,0:T(8,128)(2,1)S(1)}, u32[]{:S(2)}, u32[]{:S(2)}) collective-permute-start(bf16[1536,256]{1,0:T(8,128)(2,1)} %get-tuple-element.20.refs_1_), channel_id=1, source_target_pairs={{0,384},{128,0},{256,128},{384,256},{1,385},{129,1},{257,129},{385... | collective-permute-start | bytes 2359304 | tf_op jit(solution)/shard_map/ppermute | solution.py:288
  63.9 22.5 %collective-permute-start.3 = (bf16[1536,256]{1,0:T(8,128)(2,1)}, bf16[1536,256]{1,0:T(8,128)(2,1)S(1)}, u32[]{:S(2)}, u32[]{:S(2)}) collective-permute-start(bf16[1536,256]{1,0:T(8,128)(2,1)} %get-tuple-element.22), channel_id=1, source_target_pairs={{0,256},{128,384},{256,0},{384,128},{1,257},{129,385},{257,1},{385... | collective-permute-start | bytes 2359304 | tf_op jit(solution)/shard_map/ppermute | solution.py:288
  66.0 39.8 %all-to-all-start.1 = ((bf16[128,8,512]{2,1,0:T(8,128)(2,1)}), bf16[128,8,512]{2,1,0:T(8,128)(2,1)S(1)}, u32[]{:S(2)}, u32[]{:S(2)}) async-start(bf16[128,8,512]{2,1,0:T(8,128)(2,1)} %bitcast.17), calls=%async_computation.1 | async-start | bytes 2097152 | tf_op jit(solution)/shard_map/all_to_all | solution.py:295
  74.9 33.1 %collective-permute-start.4 = (bf16[1536,256]{1,0:T(8,128)(2,1)}, bf16[1536,256]{1,0:T(8,128)(2,1)S(1)}, u32[]{:S(2)}, u32[]{:S(2)}) collective-permute-start(bf16[1536,256]{1,0:T(8,128)(2,1)} %get-tuple-element.29), channel_id=1, source_target_pairs={{0,128},{128,256},{256,384},{384,0},{1,129},{129,257},{257,385},{3... | collective-permute-start | bytes 2359304 | tf_op jit(solution)/shard_map/ppermute | solution.py:288
  78.9 29.1 %collective-permute-start.5 = (bf16[1536,256]{1,0:T(8,128)(2,1)}, bf16[1536,256]{1,0:T(8,128)(2,1)S(1)}, u32[]{:S(2)}, u32[]{:S(2)}) collective-permute-start(bf16[1536,256]{1,0:T(8,128)(2,1)} %get-tuple-element.30), channel_id=1, source_target_pairs={{0,384},{128,0},{256,128},{384,256},{1,385},{129,1},{257,129},{385... | collective-permute-start | bytes 2359304 | tf_op jit(solution)/shard_map/ppermute | solution.py:288
  86.4 0.9 copy-start.3
  87.3 18.6 %copy-start = (bf16[24,1024]{1,0:T(8,128)(2,1)S(1)}, bf16[24,1024]{1,0:T(8,128)(2,1)}, u32[]{:S(2)}) copy-start(bf16[24,1024]{1,0:T(8,128)(2,1)} %grad_hbm.3) | copy-start | bytes 147460
  87.3 18.6 %copy-start.1 = (s32[24,8]{0,1:T(8,128)S(1)}, s32[24,8]{0,1:T(8,128)}, u32[]{:S(2)}) copy-start(s32[24,8]{0,1:T(8,128)} %param.8) | copy-start | bytes 2308
  87.3 18.6 %copy-start.2 = (f32[24,8]{0,1:T(8,128)S(1)}, f32[24,8]{0,1:T(8,128)}, u32[]{:S(2)}) copy-start(f32[24,8]{0,1:T(8,128)} %param.9) | copy-start | bytes 2308

commit v5 on v4

--- a/solution.py
+++ b/solution.py
@@ -321,8 +321,8 @@
         compiler_params=room(10),
         name="dispatch",
     )(*[held_in(x, pltpu.HBM) for x in inputs])
-    far = shift(packed, -2)
-    far_late = pl.pallas_call(
+    last = shift(packed, 1)
+    last_near = pl.pallas_call(
         lambda far_hbm, out_ref, sem: wait_all(start_all([(far_hbm, out_ref)], sem)),
         out_shape=piece_like,
         in_specs=[anywhere],
@@ -330,7 +330,7 @@
         compiler_params=room(4),
         cost_estimate=pl.CostEstimate(flops=KEEP, bytes_accessed=0, transcendentals=0),
         name="keep",
-    )(held_in(far, pltpu.HBM))
+    )(held_in(last, pltpu.HBM))
     arrived = exchange(send)
 
     back, own, grad_far, grad_next, grad_last = pl.pallas_call(
@@ -349,7 +349,7 @@
         ],
         compiler_params=room(20),
         name="expert",
-    )(arrived, held_in(packed, pltpu.HBM), far_late, shift(packed, -1), shift(packed, 1))
+    )(arrived, held_in(packed, pltpu.HBM), shift(last, 1), shift(packed, -1), last_near)
     returned = exchange(back)
     partial = pl.pallas_call(
         add_kernel,
@@ -384,7 +384,7 @@
         ],
         compiler_params=room(8),
         name="reduce",
-    )(partial, shift(grad_next, 1), shift(grad_last, -1))
+    )(partial, shift(grad_last, -1), shift(grad_next, 1))
     return mixed, grad_tokens, gate_grad.T, sum_in.reshape(1, model, 2, width), sum_out[None]
 
 

time: 110 us -> 110 us (level)
  starting transfers between devices: 47.4 us -> 45 us
  waiting for transfers between devices: 45.2 us -> 47.5 us
    ppermute x6, waiting for transfers between devices: 19.7 us -> 22.6 us  [shift(): lax.ppermute(x, 'dp', [(i, (i + by) % replicas) for i in range(replicas)])]
    ppermute x6, starting transfers between devices: 20.6 us -> 18.9 us  [shift(): lax.ppermute(x, 'dp', [(i, (i + by) % replicas) for i in range(replicas)])]
where the time goes in v5:
time: 110 us; the launch traced here: 109 us
  waiting for transfers between devices  47.5 us (43%)
  starting transfers between devices  45 us (41%)
  Pallas kernels  15.1 us (14%)
    all_to_all x2, starting transfers between devices, exchange(): x = lax.all_to_all(x, 'expert', split_axis=0, concat_axis=0, tiled=True)  26.1 us
    all_to_all x2, waiting for transfers between devices, exchange(): x = lax.all_to_all(x, 'expert', split_axis=0, concat_axis=0, tiled=True)  24.9 us
    ppermute x6, waiting for transfers between devices, shift(): lax.ppermute(x, 'dp', [(i, (i + by) % replicas) for i in range(replicas)])  22.6 us
    ppermute x6, starting transfers between devices, shift(): lax.ppermute(x, 'dp', [(i, (i + by) % replicas) for i in range(replicas)])  18.9 us
    pallas_call x1, Pallas kernels, per_device(): pl.pallas_call(lambda *refs: expert_kernel(replicas, *refs), out_shape=[p...  5.6 us
    pallas_call x1, Pallas kernels, per_device(): pl.pallas_call(dispatch_kernel, out_shape=[pltpu.HBM(piece, BF16), pltpu....  3.32 us
  transfers between devices with their start and end apart: 8, of which 5 were waited for; matrix products, arithmetic and copies ran while one was open for 0% of the time, Pallas kernels for 4%

profile of v5, /device:TPU:1, one launch (start us, length us, event | category | flops | bytes accessed | tf_op | source)
XLA Modules:
  0.0 109.3 jit_solution(12927037939406781837)
XLA Ops:
  0.6 3.3 %dispatch.1 = (bf16[1536,256]{1,0:T(8,128)(2,1)}, bf16[1024,512]{1,0:T(8,128)(2,1)}) custom-call(bf16[1024,2,128]{2,1,0:T(2,128)(2,1)} %bitcast.19, bf16[128,1024]{1,0:T(8,128)(2,1)} %bitcast.20, bf16[24,1024]{1,0:T(8,128)(2,1)} %tokens_hbm.1, bf16[24,1024]{1,0:T(8,128)(2,1)} %grad_hbm.3, s32[8,24]{1,0:T(8,128)} %bitcast.13, f32[8,24]{1,0:T(8,128)} %bitcast.15), custom_call_target="tpu_custom_call" | custom-call | tf_op jit(solution)/shard_map/dispatch/pallas_call | solution.py:310
  4.0 4.0 %collective-permute-start = (bf16[1536,256]{1,0:T(8,128)(2,1)}, bf16[1536,256]{1,0:T(8,128)(2,1)}, u32[]{:S(2)}, u32[]{:S(2)}) collective-permute-start(bf16[1536,256]{1,0:T(8,128)(2,1)} %get-tuple-element.20.refs_1_), channel_id=1, source_target_pairs={{0,128},{128,256},{256,384},{384,0},{1,129},{129,257},{257,385},{3... | collective-permute-start | bytes 2359304 | tf_op jit(solution)/shard_map/ppermute | solution.py:288
  7.9 17.9 %all-to-all-start = ((bf16[128,8,512]{2,1,0:T(8,128)(2,1)}), bf16[128,8,512]{2,1,0:T(8,128)(2,1)S(1)}, u32[]{:S(2)}, u32[]{:S(2)}) async-start(bf16[128,8,512]{2,1,0:T(8,128)(2,1)} %bitcast.18), calls=%async_computation | async-start | bytes 2097152 | tf_op jit(solution)/shard_map/all_to_all | solution.py:295
  25.8 3.4 %collective-permute-start.2 = (bf16[1536,256]{1,0:T(8,128)(2,1)}, bf16[1536,256]{1,0:T(8,128)(2,1)S(1)}, u32[]{:S(2)}, u32[]{:S(2)}) collective-permute-start(bf16[1536,256]{1,0:T(8,128)(2,1)} %get-tuple-element.20.refs_1_), channel_id=1, source_target_pairs={{0,384},{128,0},{256,128},{384,256},{1,385},{129,1},{257,129},{385... | collective-permute-start | bytes 2359304 | tf_op jit(solution)/shard_map/ppermute | solution.py:288
  29.2 0.0 collective-permute-done.far_hbm
  29.2 1.9 %collective-permute-start.1 = (bf16[1536,256]{1,0:T(8,128)(2,1)}, bf16[1536,256]{1,0:T(8,128)(2,1)S(1)}, u32[]{:S(2)}, u32[]{:S(2)}) collective-permute-start(bf16[1536,256]{1,0:T(8,128)(2,1)} %collective-permute-done.far_hbm), channel_id=1, source_target_pairs={{0,128},{128,256},{256,384},{384,0},{1,129},{129,257},{257,385},{3... | collective-permute-start | bytes 2359304 | tf_op jit(solution)/shard_map/ppermute | solution.py:288
  31.1 1.2 %keep.1.refs_4_ = bf16[1536,256]{1,0:T(8,128)(2,1)S(1)} custom-call(bf16[1536,256]{1,0:T(8,128)(2,1)} %collective-permute-done.far_hbm), custom_call_target="tpu_custom_call" | custom-call | flops 19000000512 | tf_op jit(solution)/shard_map/keep/pallas_call | solution.py:325
  32.3 13.8 %collective-permute-done.2.refs_3_ = bf16[1536,256]{1,0:T(8,128)(2,1)S(1)} collective-permute-done((bf16[1536,256]{1,0:T(8,128)(2,1)}, bf16[1536,256]{1,0:T(8,128)(2,1)S(1)}, u32[]{:S(2)}, u32[]{:S(2)}) %collective-permute-start.2) | collective-permute-done | bytes 786464 | tf_op jit(solution)/shard_map/ppermute | solution.py:288
  46.1 4.3 %collective-permute-done.1.refs_2_ = bf16[1536,256]{1,0:T(8,128)(2,1)S(1)} collective-permute-done((bf16[1536,256]{1,0:T(8,128)(2,1)}, bf16[1536,256]{1,0:T(8,128)(2,1)S(1)}, u32[]{:S(2)}, u32[]{:S(2)}) %collective-permute-start.1) | collective-permute-done | bytes 786464 | tf_op jit(solution)/shard_map/ppermute | solution.py:288
  50.4 6.3 %all-to-all-done = bf16[128,8,512]{2,1,0:T(8,128)(2,1)S(1)} async-done(((bf16[128,8,512]{2,1,0:T(8,128)(2,1)}), bf16[128,8,512]{2,1,0:T(8,128)(2,1)S(1)}, u32[]{:S(2)}, u32[]{:S(2)}) %all-to-all-start) | async-done | bytes 1048608 | tf_op jit(solution)/shard_map/all_to_all | solution.py:295
  56.7 5.6 %expert.1 = (bf16[1024,512]{1,0:T(8,128)(2,1)}, bf16[1536,256]{1,0:T(8,128)(2,1)}, bf16[1536,256]{1,0:T(8,128)(2,1)}, bf16[1536,256]{1,0:T(8,128)(2,1)}, bf16[1536,256]{1,0:T(8,128)(2,1)}) custom-call(bf16[1024,512]{1,0:T(8,128)(2,1)S(1)} %bitcast.12, bf16[1536,256]{1,0:T(8,128)(2,1)} %get-tuple-element.20.refs_1_, ...), custom_call_target="tpu_custom_call" | custom-call | tf_op jit(solution)/shard_map/expert/pallas_call | solution.py:336
  62.3 4.4 %collective-permute-start.3 = (bf16[1536,256]{1,0:T(8,128)(2,1)}, bf16[1536,256]{1,0:T(8,128)(2,1)S(1)}, u32[]{:S(2)}, u32[]{:S(2)}) collective-permute-start(bf16[1536,256]{1,0:T(8,128)(2,1)} %get-tuple-element.22), channel_id=1, source_target_pairs={{0,256},{128,384},{256,0},{384,128},{1,257},{129,385},{257,1},{385... | collective-permute-start | bytes 2359304 | tf_op jit(solution)/shard_map/ppermute | solution.py:288
  66.7 8.2 %all-to-all-start.1 = ((bf16[128,8,512]{2,1,0:T(8,128)(2,1)}), bf16[128,8,512]{2,1,0:T(8,128)(2,1)S(1)}, u32[]{:S(2)}, u32[]{:S(2)}) async-start(bf16[128,8,512]{2,1,0:T(8,128)(2,1)} %bitcast.17), calls=%async_computation.1 | async-start | bytes 2097152 | tf_op jit(solution)/shard_map/all_to_all | solution.py:295
  74.9 2.8 %collective-permute-start.4 = (bf16[1536,256]{1,0:T(8,128)(2,1)}, bf16[1536,256]{1,0:T(8,128)(2,1)S(1)}, u32[]{:S(2)}, u32[]{:S(2)}) collective-permute-start(bf16[1536,256]{1,0:T(8,128)(2,1)} %get-tuple-element.29), channel_id=1, source_target_pairs={{0,384},{128,0},{256,128},{384,256},{1,385},{129,1},{257,129},{385... | collective-permute-start | bytes 2359304 | tf_op jit(solution)/shard_map/ppermute | solution.py:288
  77.7 2.5 %collective-permute-start.5 = (bf16[1536,256]{1,0:T(8,128)(2,1)}, bf16[1536,256]{1,0:T(8,128)(2,1)S(1)}, u32[]{:S(2)}, u32[]{:S(2)}) collective-permute-start(bf16[1536,256]{1,0:T(8,128)(2,1)} %get-tuple-element.30), channel_id=1, source_target_pairs={{0,128},{128,256},{256,384},{384,0},{1,129},{129,257},{257,385},{3... | collective-permute-start | bytes 2359304 | tf_op jit(solution)/shard_map/ppermute | solution.py:288
  80.2 4.5 %collective-permute-done.3.second_hbm = bf16[1536,256]{1,0:T(8,128)(2,1)S(1)} collective-permute-done((bf16[1536,256]{1,0:T(8,128)(2,1)}, bf16[1536,256]{1,0:T(8,128)(2,1)S(1)}, u32[]{:S(2)}, u32[]{:S(2)}) %collective-permute-start.3) | collective-permute-done | bytes 786464 | tf_op jit(solution)/shard_map/ppermute | solution.py:288
  84.8 0.0 copy-start.3
  84.8 0.9 copy-done.3
  85.7 0.0 copy-start
  85.7 0.0 copy-start.1
  85.7 0.0 copy-start.2
  85.7 1.6 %add.1.refs_0_ = bf16[1536,256]{1,0:T(8,128)(2,1)S(1)} custom-call(bf16[1536,256]{1,0:T(8,128)(2,1)} %get-tuple-element.21.first_hbm, bf16[1536,256]{1,0:T(8,128)(2,1)} %copy-done.3), custom_call_target="tpu_custom_call" | custom-call | flops 99999997952 | tf_op jit(solution)/shard_map/add/pallas_call | solution.py:354
  87.3 18.6 %all-to-all-done.1 = bf16[128,8,512]{2,1,0:T(8,128)(2,1)S(1)} async-done(((bf16[128,8,512]{2,1,0:T(8,128)(2,1)}), bf16[128,8,512]{2,1,0:T(8,128)(2,1)S(1)}, u32[]{:S(2)}, u32[]{:S(2)}) %all-to-all-start.1) | async-done | bytes 1048608 | tf_op jit(solution)/shard_map/all_to_all | solution.py:295
  105.9 0.0 copy-done
  105.9 0.0 copy-done.1
  105.9 0.0 copy-done.2
  105.9 2.1 %combine.1 = (bf16[24,1024]{1,0:T(8,128)(2,1)}, bf16[24,1024]{1,0:T(8,128)(2,1)}, f32[8,24]{1,0:T(8,128)}) custom-call(bf16[1024,512]{1,0:T(8,128)(2,1)S(1)} %bitcast.11, bf16[24,1024]{1,0:T(8,128)(2,1)S(1)} %copy-done, s32[8,24]{1,0:T(8,128)S(1)} %bitcast.14, f32[8,24]{1,0:T(8,128)S(1)} %bitcast.16), custom_call_target="tpu_custom_call" | custom-call | tf_op jit(solution)/shard_map/combine/pallas_call | solution.py:363
  108.0 0.0 collective-permute-done.4.refs_1_
  108.0 0.0 collective-permute-done.5.refs_2_
  108.0 1.3 %reduce.1 = (f32[2048,128]{1,0:T(8,128)}, f32[128,1024]{1,0:T(8,128)}) custom-call(bf16[1536,256]{1,0:T(8,128)(2,1)S(1)} %add.1.refs_0_, bf16[1536,256]{1,0:T(8,128)(2,1)S(1)} %collective-permute-done.4.refs_1_, bf16[1536,256]{1,0:T(8,128)(2,1)S(1)} %collective-permute-done.5.refs_2_), custom_call_target="tpu_custom_call" | custom-call | tf_op jit(solution)/shard_map/reduce/pallas_call | solution.py:379
Async XLA Ops:
  4.0 25.2 %collective-permute-start = (bf16[1536,256]{1,0:T(8,128)(2,1)}, bf16[1536,256]{1,0:T(8,128)(2,1)}, u32[]{:S(2)}, u32[]{:S(2)}) collective-permute-start(bf16[1536,256]{1,0:T(8,128)(2,1)} %get-tuple-element.20.refs_1_), channel_id=1, source_target_pairs={{0,128},{128,256},{256,384},{384,0},{1,129},{129,257},{257,385},{3... | collective-permute-start | bytes 2359304 | tf_op jit(solution)/shard_map/ppermute | solution.py:288
  7.9 48.8 %all-to-all-start = ((bf16[128,8,512]{2,1,0:T(8,128)(2,1)}), bf16[128,8,512]{2,1,0:T(8,128)(2,1)S(1)}, u32[]{:S(2)}, u32[]{:S(2)}) async-start(bf16[128,8,512]{2,1,0:T(8,128)(2,1)} %bitcast.18), calls=%async_computation | async-start | bytes 2097152 | tf_op jit(solution)/shard_map/all_to_all | solution.py:295
  25.8 20.3 %collective-permute-start.2 = (bf16[1536,256]{1,0:T(8,128)(2,1)}, bf16[1536,256]{1,0:T(8,128)(2,1)S(1)}, u32[]{:S(2)}, u32[]{:S(2)}) collective-permute-start(bf16[1536,256]{1,0:T(8,128)(2,1)} %get-tuple-element.20.refs_1_), channel_id=1, source_target_pairs={{0,384},{128,0},{256,128},{384,256},{1,385},{129,1},{257,129},{385... | collective-permute-start | bytes 2359304 | tf_op jit(solution)/shard_map/ppermute | solution.py:288
  29.2 21.2 %collective-permute-start.1 = (bf16[1536,256]{1,0:T(8,128)(2,1)}, bf16[1536,256]{1,0:T(8,128)(2,1)S(1)}, u32[]{:S(2)}, u32[]{:S(2)}) collective-permute-start(bf16[1536,256]{1,0:T(8,128)(2,1)} %collective-permute-done.far_hbm), channel_id=1, source_target_pairs={{0,128},{128,256},{256,384},{384,0},{1,129},{129,257},{257,385},{3... | collective-permute-start | bytes 2359304 | tf_op jit(solution)/shard_map/ppermute | solution.py:288
  62.3 22.5 %collective-permute-start.3 = (bf16[1536,256]{1,0:T(8,128)(2,1)}, bf16[1536,256]{1,0:T(8,128)(2,1)S(1)}, u32[]{:S(2)}, u32[]{:S(2)}) collective-permute-start(bf16[1536,256]{1,0:T(8,128)(2,1)} %get-tuple-element.22), channel_id=1, source_target_pairs={{0,256},{128,384},{256,0},{384,128},{1,257},{129,385},{257,1},{385... | collective-permute-start | bytes 2359304 | tf_op jit(solution)/shard_map/ppermute | solution.py:288
  66.7 39.2 %all-to-all-start.1 = ((bf16[128,8,512]{2,1,0:T(8,128)(2,1)}), bf16[128,8,512]{2,1,0:T(8,128)(2,1)S(1)}, u32[]{:S(2)}, u32[]{:S(2)}) async-start(bf16[128,8,512]{2,1,0:T(8,128)(2,1)} %bitcast.17), calls=%async_computation.1 | async-start | bytes 2097152 | tf_op jit(solution)/shard_map/all_to_all | solution.py:295
  74.9 33.1 %collective-permute-start.4 = (bf16[1536,256]{1,0:T(8,128)(2,1)}, bf16[1536,256]{1,0:T(8,128)(2,1)S(1)}, u32[]{:S(2)}, u32[]{:S(2)}) collective-permute-start(bf16[1536,256]{1,0:T(8,128)(2,1)} %get-tuple-element.29), channel_id=1, source_target_pairs={{0,384},{128,0},{256,128},{384,256},{1,385},{129,1},{257,129},{385... | collective-permute-start | bytes 2359304 | tf_op jit(solution)/shard_map/ppermute | solution.py:288
  77.7 30.3 %collective-permute-start.5 = (bf16[1536,256]{1,0:T(8,128)(2,1)}, bf16[1536,256]{1,0:T(8,128)(2,1)S(1)}, u32[]{:S(2)}, u32[]{:S(2)}) collective-permute-start(bf16[1536,256]{1,0:T(8,128)(2,1)} %get-tuple-element.30), channel_id=1, source_target_pairs={{0,128},{128,256},{256,384},{384,0},{1,129},{129,257},{257,385},{3... | collective-permute-start | bytes 2359304 | tf_op jit(solution)/shard_map/ppermute | solution.py:288
  84.8 0.9 copy-start.3
  85.7 20.2 %copy-start = (bf16[24,1024]{1,0:T(8,128)(2,1)S(1)}, bf16[24,1024]{1,0:T(8,128)(2,1)}, u32[]{:S(2)}) copy-start(bf16[24,1024]{1,0:T(8,128)(2,1)} %grad_hbm.3) | copy-start | bytes 147460
  85.7 20.2 %copy-start.1 = (s32[24,8]{0,1:T(8,128)S(1)}, s32[24,8]{0,1:T(8,128)}, u32[]{:S(2)}) copy-start(s32[24,8]{0,1:T(8,128)} %param.8) | copy-start | bytes 2308
  85.7 20.2 %copy-start.2 = (f32[24,8]{0,1:T(8,128)S(1)}, f32[24,8]{0,1:T(8,128)}, u32[]{:S(2)}) copy-start(f32[24,8]{0,1:T(8,128)} %param.9) | copy-start | bytes 2308

commit v6 on v5

--- a/solution.py
+++ b/solution.py
@@ -173,18 +173,20 @@
 def expert_kernel(
     pieces, wire_hbm, *refs
 ):
-    sources, back_hbm, grads_hbm = refs[:pieces], refs[pieces], refs[pieces + 1 : 2 * pieces + 1]
-    grads = refs[2 * pieces + 1 : 3 * pieces + 1]
+    sources = refs[:pieces]
     (
-        in_ref, out_ref, wire_ref, rows_ref, grad_rows_ref, hidden_ref, grad_pre_ref, sem, weights_sem, grad_sem
-    ) = refs[3 * pieces + 1 :]
-    wide = grads[0].shape[1]
+        back_hbm, rows_hbm, grad_rows_hbm, hidden_hbm, grad_pre_hbm, grad_hbm,
+        grad_ref, in_ref, out_ref, wire_ref, rows_ref, grad_rows_ref, hidden_ref, grad_pre_ref,
+        sem, weights_sem, grad_sem, keep_sem,
+    ) = refs[pieces:]
+    wide = grad_ref.shape[1]
     width = wide // 2
     arriving = pltpu.make_async_copy(wire_hbm, wire_ref, sem)
     arriving.start()
     weights = start_all(assembly(sources, in_ref, out_ref), weights_sem)
     arriving.wait()
     unweave_blocks(wire_ref, rows_ref, grad_rows_ref)
+    keeping = start_all([(rows_ref, rows_hbm), (grad_rows_ref, grad_rows_hbm)], keep_sem)
     wait_all(weights)
     rows = rows_ref[...]
     grad_rows = grad_rows_ref[...]
@@ -202,17 +204,27 @@
         grad_pre_ref[:, r * wide + width : (r + 1) * wide] = (back_part * activated).astype(BF16)
     hidden = hidden_ref[...]
     grad_pre = grad_pre_ref[...]
-    order = (1, 2, 3, 0)
-    for r in order:
-        weight_grads(rows, grad_rows, hidden, grad_pre, r, grads[r])
-    leaving = start_all([(grads[r], grads_hbm[r]) for r in order], grad_sem)
+    for i, pair in enumerate([(hidden_ref, hidden_hbm), (grad_pre_ref, grad_pre_hbm)]):
+        keeping.append(pltpu.make_async_copy(*pair, keep_sem.at[2 + i]))
+        keeping[-1].start()
+    weight_grads(rows, grad_rows, hidden, grad_pre, 1, grad_ref)
+    leaving = pltpu.make_async_copy(grad_ref, grad_hbm, grad_sem)
+    leaving.start()
     result = jnp.dot(hidden, out_ref[...], preferred_element_type=F32).astype(BF16)
     dx = lax.dot_general(grad_pre, in_ref[...], LAST, preferred_element_type=F32).astype(BF16)
     weave_blocks(result, dx, wire_ref)
     sending = pltpu.make_async_copy(wire_ref, back_hbm, sem)
     sending.start()
     sending.wait()
-    wait_all(leaving)
+    leaving.wait()
+    wait_all(keeping)
+
+
+def weights_kernel(rows_ref, grad_rows_ref, hidden_ref, grad_pre_ref, own_ref, next_ref, last_ref):
+    operands = rows_ref[...], grad_rows_ref[...], hidden_ref[...], grad_pre_ref[...]
+    weight_grads(*operands, 3, last_ref)
+    weight_grads(*operands, 2, next_ref)
+    weight_grads(*operands, 0, own_ref)
 
 
 def combine_kernel(
@@ -333,23 +345,32 @@
     )(held_in(last, pltpu.HBM))
     arrived = exchange(send)
 
-    back, own, grad_far, grad_next, grad_last = pl.pallas_call(
+    back, rows, grad_rows, hidden, grad_pre, grad_far = pl.pallas_call(
         lambda *refs: expert_kernel(replicas, *refs),
-        out_shape=[pltpu.HBM(wire.shape, BF16)] + [pltpu.HBM(piece, BF16)] * replicas,
+        out_shape=[
+            pltpu.HBM(x.shape, BF16) for x in (wire, rows_like, rows_like, hidden_like, grad_pre_like, piece_like)
+        ],
         in_specs=[in_hbm] + [anywhere] * replicas,
-        out_specs=[in_hbm] * (1 + replicas),
-        scratch_shapes=[piece_like] * replicas
-        + [
+        out_specs=[in_hbm] * 6,
+        scratch_shapes=[
+            piece_like,
             pltpu.VMEM((model, replicas * wide), BF16),
             pltpu.VMEM((replicas * width, model), BF16),
             wire_like, rows_like, rows_like, hidden_like, grad_pre_like,
             pltpu.SemaphoreType.DMA,
             pltpu.SemaphoreType.DMA((replicas * lines,)),
-            pltpu.SemaphoreType.DMA((replicas,)),
+            pltpu.SemaphoreType.DMA,
+            pltpu.SemaphoreType.DMA((4,)),
         ],
         compiler_params=room(20),
         name="expert",
     )(arrived, held_in(packed, pltpu.HBM), shift(last, 1), shift(packed, -1), last_near)
+    own, grad_next, grad_last = pl.pallas_call(
+        weights_kernel,
+        out_shape=[jax.ShapeDtypeStruct(piece, BF16)] * 3,
+        compiler_params=room(10),
+        name="weights",
+    )(rows, grad_rows, hidden, grad_pre)
     returned = exchange(back)
     partial = pl.pallas_call(
         add_kernel,

time: 110 us -> 110 us (level)
  waiting for transfers between devices: 47.5 us -> 45.9 us
    ppermute x6, waiting for transfers between devices: 22.6 us -> 20.1 us  [shift(): lax.ppermute(x, 'dp', [(i, (i + by) % replicas) for i in range(replicas)])]
    pallas_call x0 -> x1, Pallas kernels: none -> 1.6 us  [per_device(): pl.pallas_call(weights_kernel, out_shape=[jax.ShapeDtypeStruct(piece, BF1...]
  transfers between devices with their start and end apart: 8 -> 8, of which waited for: 5 -> 5; matrix products, arithmetic and copies ran while one was open for 0% -> 0% of each run, Pallas kernels for 4% -> 6%
where the time goes in v6:
time: 110 us; the launch traced here: 109 us
  waiting for transfers between devices  45.9 us (42%)
  starting transfers between devices  45.1 us (41%)
  Pallas kernels  16.2 us (15%)
    all_to_all x2, starting transfers between devices, exchange(): x = lax.all_to_all(x, 'expert', split_axis=0, concat_axis=0, tiled=True)  26.3 us
    all_to_all x2, waiting for transfers between devices, exchange(): x = lax.all_to_all(x, 'expert', split_axis=0, concat_axis=0, tiled=True)  25.9 us
    ppermute x6, waiting for transfers between devices, shift(): lax.ppermute(x, 'dp', [(i, (i + by) % replicas) for i in range(replicas)])  20.1 us
    ppermute x6, starting transfers between devices, shift(): lax.ppermute(x, 'dp', [(i, (i + by) % replicas) for i in range(replicas)])  18.9 us
    pallas_call x1, Pallas kernels, per_device(): pl.pallas_call(lambda *refs: expert_kernel(replicas, *refs), out_shape=[p...  5.04 us
    pallas_call x1, Pallas kernels, per_device(): pl.pallas_call(dispatch_kernel, out_shape=[pltpu.HBM(piece, BF16), pltpu....  3.34 us
  transfers between devices with their start and end apart: 8, of which 5 were waited for; matrix products, arithmetic and copies ran while one was open for 0% of the time, Pallas kernels for 6%

profile of v6, /device:TPU:1, one launch (start us, length us, event | category | flops | bytes accessed | tf_op | source)
XLA Modules:
  0.0 109.0 jit_solution(11336748962906090255)
XLA Ops:
  0.6 3.3 %dispatch.1 = (bf16[1536,256]{1,0:T(8,128)(2,1)}, bf16[1024,512]{1,0:T(8,128)(2,1)}) custom-call(bf16[1024,2,128]{2,1,0:T(2,128)(2,1)} %bitcast.19, bf16[128,1024]{1,0:T(8,128)(2,1)} %bitcast.20, bf16[24,1024]{1,0:T(8,128)(2,1)} %tokens_hbm.1, bf16[24,1024]{1,0:T(8,128)(2,1)} %grad_hbm.3, s32[8,24]{1,0:T(8,128)} %bitcast.13, f32[8,24]{1,0:T(8,128)} %bitcast.15), custom_call_target="tpu_custom_call" | custom-call | tf_op jit(solution)/shard_map/dispatch/pallas_call | solution.py:322
  4.0 4.0 %collective-permute-start = (bf16[1536,256]{1,0:T(8,128)(2,1)}, bf16[1536,256]{1,0:T(8,128)(2,1)}, u32[]{:S(2)}, u32[]{:S(2)}) collective-permute-start(bf16[1536,256]{1,0:T(8,128)(2,1)} %get-tuple-element.24.refs_1_), channel_id=1, source_target_pairs={{0,128},{128,256},{256,384},{384,0},{1,129},{129,257},{257,385},{3... | collective-permute-start | bytes 2359304 | tf_op jit(solution)/shard_map/ppermute | solution.py:300
  7.9 17.9 %all-to-all-start = ((bf16[128,8,512]{2,1,0:T(8,128)(2,1)}), bf16[128,8,512]{2,1,0:T(8,128)(2,1)S(1)}, u32[]{:S(2)}, u32[]{:S(2)}) async-start(bf16[128,8,512]{2,1,0:T(8,128)(2,1)} %bitcast.18), calls=%async_computation | async-start | bytes 2097152 | tf_op jit(solution)/shard_map/all_to_all | solution.py:307
  25.8 3.4 %collective-permute-start.2 = (bf16[1536,256]{1,0:T(8,128)(2,1)}, bf16[1536,256]{1,0:T(8,128)(2,1)S(1)}, u32[]{:S(2)}, u32[]{:S(2)}) collective-permute-start(bf16[1536,256]{1,0:T(8,128)(2,1)} %get-tuple-element.24.refs_1_), channel_id=1, source_target_pairs={{0,384},{128,0},{256,128},{384,256},{1,385},{129,1},{257,129},{385... | collective-permute-start | bytes 2359304 | tf_op jit(solution)/shard_map/ppermute | solution.py:300
  29.2 0.0 collective-permute-done.far_hbm
  29.2 1.9 %collective-permute-start.1 = (bf16[1536,256]{1,0:T(8,128)(2,1)}, bf16[1536,256]{1,0:T(8,128)(2,1)S(1)}, u32[]{:S(2)}, u32[]{:S(2)}) collective-permute-start(bf16[1536,256]{1,0:T(8,128)(2,1)} %collective-permute-done.far_hbm), channel_id=1, source_target_pairs={{0,128},{128,256},{256,384},{384,0},{1,129},{129,257},{257,385},{3... | collective-permute-start | bytes 2359304 | tf_op jit(solution)/shard_map/ppermute | solution.py:300
  31.1 1.2 %keep.1.refs_4_ = bf16[1536,256]{1,0:T(8,128)(2,1)S(1)} custom-call(bf16[1536,256]{1,0:T(8,128)(2,1)} %collective-permute-done.far_hbm), custom_call_target="tpu_custom_call" | custom-call | flops 19000000512 | tf_op jit(solution)/shard_map/keep/pallas_call | solution.py:337
  32.3 13.8 %collective-permute-done.2.refs_3_ = bf16[1536,256]{1,0:T(8,128)(2,1)S(1)} collective-permute-done((bf16[1536,256]{1,0:T(8,128)(2,1)}, bf16[1536,256]{1,0:T(8,128)(2,1)S(1)}, u32[]{:S(2)}, u32[]{:S(2)}) %collective-permute-start.2) | collective-permute-done | bytes 786464 | tf_op jit(solution)/shard_map/ppermute | solution.py:300
  46.1 4.3 %collective-permute-done.1.refs_2_ = bf16[1536,256]{1,0:T(8,128)(2,1)S(1)} collective-permute-done((bf16[1536,256]{1,0:T(8,128)(2,1)}, bf16[1536,256]{1,0:T(8,128)(2,1)S(1)}, u32[]{:S(2)}, u32[]{:S(2)}) %collective-permute-start.1) | collective-permute-done | bytes 786464 | tf_op jit(solution)/shard_map/ppermute | solution.py:300
  50.4 6.3 %all-to-all-done = bf16[128,8,512]{2,1,0:T(8,128)(2,1)S(1)} async-done(((bf16[128,8,512]{2,1,0:T(8,128)(2,1)}), bf16[128,8,512]{2,1,0:T(8,128)(2,1)S(1)}, u32[]{:S(2)}, u32[]{:S(2)}) %all-to-all-start) | async-done | bytes 1048608 | tf_op jit(solution)/shard_map/all_to_all | solution.py:307
  56.7 5.0 %expert.1 = (bf16[1024,512]{1,0:T(8,128)(2,1)}, bf16[256,1024]{1,0:T(8,128)(2,1)}, bf16[256,1024]{1,0:T(8,128)(2,1)}, bf16[256,512]{1,0:T(8,128)(2,1)}, bf16[256...) custom-call(bf16[1024,512]{1,0:T(8,128)(2,1)S(1)} %bitcast.12, bf16[1536,256]{1,0:T(8,128)(2,1)} %get-tuple-element.24.refs_1_, ...), custom_call_target="tpu_custom_call" | custom-call | tf_op jit(solution)/shard_map/expert/pallas_call | solution.py:348
  61.8 4.4 %collective-permute-start.3 = (bf16[1536,256]{1,0:T(8,128)(2,1)}, bf16[1536,256]{1,0:T(8,128)(2,1)}, u32[]{:S(2)}, u32[]{:S(2)}) collective-permute-start(bf16[1536,256]{1,0:T(8,128)(2,1)} %get-tuple-element.30), channel_id=1, source_target_pairs={{0,256},{128,384},{256,0},{384,128},{1,257},{129,385},{257,1},{385... | collective-permute-start | bytes 2359304 | tf_op jit(solution)/shard_map/ppermute | solution.py:300
  66.1 0.0 copy-start
  66.2 0.0 copy-start.1
  66.2 0.0 copy-start.2
  66.2 0.0 copy-start.3
  66.2 8.4 %all-to-all-start.1 = ((bf16[128,8,512]{2,1,0:T(8,128)(2,1)}), bf16[128,8,512]{2,1,0:T(8,128)(2,1)S(1)}, u32[]{:S(2)}, u32[]{:S(2)}) async-start(bf16[128,8,512]{2,1,0:T(8,128)(2,1)} %bitcast.17), calls=%async_computation.1 | async-start | bytes 2097152 | tf_op jit(solution)/shard_map/all_to_all | solution.py:307
  74.6 0.0 copy-done
  74.6 0.0 copy-done.1
  74.6 0.0 copy-done.2
  74.6 0.0 copy-done.3
  74.6 1.6 %weights.1 = (bf16[1536,256]{1,0:T(8,128)(2,1)S(1)}, bf16[1536,256]{1,0:T(8,128)(2,1)}, bf16[1536,256]{1,0:T(8,128)(2,1)}) custom-call(bf16[256,1024]{1,0:T(8,128)(2,1)S(1)} %copy-done, bf16[256,1024]{1,0:T(8,128)(2,1)S(1)} %copy-done.1, bf16[256,512]{1,0:T(8,128)(2,1)S(1)} %copy-done.3, bf16[256,1024]{1,0:T(8,128)(2,1)S(1)} %copy-done.2), custom_call_target="tpu_custom_call" | custom-call | tf_op jit(solution)/shard_map/weights/pallas_call | solution.py:368
  76.2 0.0 copy-start.7
  76.2 0.9 copy-done.7
  77.1 2.8 %collective-permute-start.4 = (bf16[1536,256]{1,0:T(8,128)(2,1)}, bf16[1536,256]{1,0:T(8,128)(2,1)S(1)}, u32[]{:S(2)}, u32[]{:S(2)}) collective-permute-start(bf16[1536,256]{1,0:T(8,128)(2,1)} %get-tuple-element.37), channel_id=1, source_target_pairs={{0,384},{128,0},{256,128},{384,256},{1,385},{129,1},{257,129},{385... | collective-permute-start | bytes 2359304 | tf_op jit(solution)/shard_map/ppermute | solution.py:300
  79.9 2.5 %collective-permute-start.5 = (bf16[1536,256]{1,0:T(8,128)(2,1)}, bf16[1536,256]{1,0:T(8,128)(2,1)S(1)}, u32[]{:S(2)}, u32[]{:S(2)}) collective-permute-start(bf16[1536,256]{1,0:T(8,128)(2,1)} %get-tuple-element.38), channel_id=1, source_target_pairs={{0,128},{128,256},{256,384},{384,0},{1,129},{129,257},{257,385},{3... | collective-permute-start | bytes 2359304 | tf_op jit(solution)/shard_map/ppermute | solution.py:300
  82.4 2.0 %collective-permute-done.3.second_hbm = bf16[1536,256]{1,0:T(8,128)(2,1)} collective-permute-done((bf16[1536,256]{1,0:T(8,128)(2,1)}, bf16[1536,256]{1,0:T(8,128)(2,1)}, u32[]{:S(2)}, u32[]{:S(2)}) %collective-permute-start.3) | collective-permute-done | bytes 786464 | tf_op jit(solution)/shard_map/ppermute | solution.py:300
  84.4 0.0 copy-start.4
  84.4 0.0 copy-start.5
  84.4 0.0 copy-start.6
  84.4 1.6 %add.1.refs_0_ = bf16[1536,256]{1,0:T(8,128)(2,1)S(1)} custom-call(bf16[1536,256]{1,0:T(8,128)(2,1)} %copy-done.7, bf16[1536,256]{1,0:T(8,128)(2,1)} %collective-permute-done.3.second_hbm), custom_call_target="tpu_custom_call" | custom-call | flops 99999997952 | tf_op jit(solution)/shard_map/add/pallas_call | solution.py:375
  85.9 19.5 %all-to-all-done.1 = bf16[128,8,512]{2,1,0:T(8,128)(2,1)S(1)} async-done(((bf16[128,8,512]{2,1,0:T(8,128)(2,1)}), bf16[128,8,512]{2,1,0:T(8,128)(2,1)S(1)}, u32[]{:S(2)}, u32[]{:S(2)}) %all-to-all-start.1) | async-done | bytes 1048608 | tf_op jit(solution)/shard_map/all_to_all | solution.py:307
  105.5 0.0 copy-done.4
  105.5 0.0 copy-done.5
  105.5 0.0 copy-done.6
  105.5 2.1 %combine.1 = (bf16[24,1024]{1,0:T(8,128)(2,1)}, bf16[24,1024]{1,0:T(8,128)(2,1)}, f32[8,24]{1,0:T(8,128)}) custom-call(bf16[1024,512]{1,0:T(8,128)(2,1)S(1)} %bitcast.11, bf16[24,1024]{1,0:T(8,128)(2,1)S(1)} %copy-done.4, s32[8,24]{1,0:T(8,128)S(1)} %bitcast.14, f32[8,24]{1,0:T(8,128)S(1)} %bitcast.16), custom_call_target="tpu_custom_call" | custom-call | tf_op jit(solution)/shard_map/combine/pallas_call | solution.py:384
  107.6 0.0 collective-permute-done.4.refs_1_
  107.6 0.0 collective-permute-done.5.refs_2_
  107.7 1.3 %reduce.1 = (f32[2048,128]{1,0:T(8,128)}, f32[128,1024]{1,0:T(8,128)}) custom-call(bf16[1536,256]{1,0:T(8,128)(2,1)S(1)} %add.1.refs_0_, bf16[1536,256]{1,0:T(8,128)(2,1)S(1)} %collective-permute-done.4.refs_1_, bf16[1536,256]{1,0:T(8,128)(2,1)S(1)} %collective-permute-done.5.refs_2_), custom_call_target="tpu_custom_call" | custom-call | tf_op jit(solution)/shard_map/reduce/pallas_call | solution.py:400
Async XLA Ops:
  4.0 25.2 %collective-permute-start = (bf16[1536,256]{1,0:T(8,128)(2,1)}, bf16[1536,256]{1,0:T(8,128)(2,1)}, u32[]{:S(2)}, u32[]{:S(2)}) collective-permute-start(bf16[1536,256]{1,0:T(8,128)(2,1)} %get-tuple-element.24.refs_1_), channel_id=1, source_target_pairs={{0,128},{128,256},{256,384},{384,0},{1,129},{129,257},{257,385},{3... | collective-permute-start | bytes 2359304 | tf_op jit(solution)/shard_map/ppermute | solution.py:300
  7.9 48.8 %all-to-all-start = ((bf16[128,8,512]{2,1,0:T(8,128)(2,1)}), bf16[128,8,512]{2,1,0:T(8,128)(2,1)S(1)}, u32[]{:S(2)}, u32[]{:S(2)}) async-start(bf16[128,8,512]{2,1,0:T(8,128)(2,1)} %bitcast.18), calls=%async_computation | async-start | bytes 2097152 | tf_op jit(solution)/shard_map/all_to_all | solution.py:307
  25.8 20.3 %collective-permute-start.2 = (bf16[1536,256]{1,0:T(8,128)(2,1)}, bf16[1536,256]{1,0:T(8,128)(2,1)S(1)}, u32[]{:S(2)}, u32[]{:S(2)}) collective-permute-start(bf16[1536,256]{1,0:T(8,128)(2,1)} %get-tuple-element.24.refs_1_), channel_id=1, source_target_pairs={{0,384},{128,0},{256,128},{384,256},{1,385},{129,1},{257,129},{385... | collective-permute-start | bytes 2359304 | tf_op jit(solution)/shard_map/ppermute | solution.py:300
  29.2 21.2 %collective-permute-start.1 = (bf16[1536,256]{1,0:T(8,128)(2,1)}, bf16[1536,256]{1,0:T(8,128)(2,1)S(1)}, u32[]{:S(2)}, u32[]{:S(2)}) collective-permute-start(bf16[1536,256]{1,0:T(8,128)(2,1)} %collective-permute-done.far_hbm), channel_id=1, source_target_pairs={{0,128},{128,256},{256,384},{384,0},{1,129},{129,257},{257,385},{3... | collective-permute-start | bytes 2359304 | tf_op jit(solution)/shard_map/ppermute | solution.py:300
  61.8 22.6 %collective-permute-start.3 = (bf16[1536,256]{1,0:T(8,128)(2,1)}, bf16[1536,256]{1,0:T(8,128)(2,1)}, u32[]{:S(2)}, u32[]{:S(2)}) collective-permute-start(bf16[1536,256]{1,0:T(8,128)(2,1)} %get-tuple-element.30), channel_id=1, source_target_pairs={{0,256},{128,384},{256,0},{384,128},{1,257},{129,385},{257,1},{385... | collective-permute-start | bytes 2359304 | tf_op jit(solution)/shard_map/ppermute | solution.py:300
  66.1 8.4 %copy-start = (bf16[256,1024]{1,0:T(8,128)(2,1)S(1)}, bf16[256,1024]{1,0:T(8,128)(2,1)}, u32[]{:S(2)}) copy-start(bf16[256,1024]{1,0:T(8,128)(2,1)} %get-tuple-element.25.rows_ref) | copy-start | bytes 1572868
  66.2 8.4 %copy-start.1 = (bf16[256,1024]{1,0:T(8,128)(2,1)S(1)}, bf16[256,1024]{1,0:T(8,128)(2,1)}, u32[]{:S(2)}) copy-start(bf16[256,1024]{1,0:T(8,128)(2,1)} %get-tuple-element.26.grad_rows_ref) | copy-start | bytes 1572868
  66.2 8.4 %copy-start.2 = (bf16[256,1024]{1,0:T(8,128)(2,1)S(1)}, bf16[256,1024]{1,0:T(8,128)(2,1)}, u32[]{:S(2)}) copy-start(bf16[256,1024]{1,0:T(8,128)(2,1)} %get-tuple-element.28.grad_pre_ref) | copy-start | bytes 1572868
  66.2 8.4 %copy-start.3 = (bf16[256,512]{1,0:T(8,128)(2,1)S(1)}, bf16[256,512]{1,0:T(8,128)(2,1)}, u32[]{:S(2)}) copy-start(bf16[256,512]{1,0:T(8,128)(2,1)} %get-tuple-element.27.hidden_ref) | copy-start | bytes 786436
  66.2 39.3 %all-to-all-start.1 = ((bf16[128,8,512]{2,1,0:T(8,128)(2,1)}), bf16[128,8,512]{2,1,0:T(8,128)(2,1)S(1)}, u32[]{:S(2)}, u32[]{:S(2)}) async-start(bf16[128,8,512]{2,1,0:T(8,128)(2,1)} %bitcast.17), calls=%async_computation.1 | async-start | bytes 2097152 | tf_op jit(solution)/shard_map/all_to_all | solution.py:307
  76.2 0.9 copy-start.7
  77.1 30.5 %collective-permute-start.4 = (bf16[1536,256]{1,0:T(8,128)(2,1)}, bf16[1536,256]{1,0:T(8,128)(2,1)S(1)}, u32[]{:S(2)}, u32[]{:S(2)}) collective-permute-start(bf16[1536,256]{1,0:T(8,128)(2,1)} %get-tuple-element.37), channel_id=1, source_target_pairs={{0,384},{128,0},{256,128},{384,256},{1,385},{129,1},{257,129},{385... | collective-permute-start | bytes 2359304 | tf_op jit(solution)/shard_map/ppermute | solution.py:300
  79.9 27.8 %collective-permute-start.5 = (bf16[1536,256]{1,0:T(8,128)(2,1)}, bf16[1536,256]{1,0:T(8,128)(2,1)S(1)}, u32[]{:S(2)}, u32[]{:S(2)}) collective-permute-start(bf16[1536,256]{1,0:T(8,128)(2,1)} %get-tuple-element.38), channel_id=1, source_target_pairs={{0,128},{128,256},{256,384},{384,0},{1,129},{129,257},{257,385},{3... | collective-permute-start | bytes 2359304 | tf_op jit(solution)/shard_map/ppermute | solution.py:300
  84.4 21.1 %copy-start.4 = (bf16[24,1024]{1,0:T(8,128)(2,1)S(1)}, bf16[24,1024]{1,0:T(8,128)(2,1)}, u32[]{:S(2)}) copy-start(bf16[24,1024]{1,0:T(8,128)(2,1)} %grad_hbm.3) | copy-start | bytes 147460
  84.4 21.1 %copy-start.5 = (s32[24,8]{0,1:T(8,128)S(1)}, s32[24,8]{0,1:T(8,128)}, u32[]{:S(2)}) copy-start(s32[24,8]{0,1:T(8,128)} %param.8) | copy-start | bytes 2308
  84.4 21.1 %copy-start.6 = (f32[24,8]{0,1:T(8,128)S(1)}, f32[24,8]{0,1:T(8,128)}, u32[]{:S(2)}) copy-start(f32[24,8]{0,1:T(8,128)} %param.9) | copy-start | bytes 2308
